TPU v7x, 32 devices: a whole 2x2x4 slice. The times are simulated.
32 devices in a mesh: row: 4 (over y, x), col: 8 (over z, core).
Axes of the slice: x: 2, y: 2, z: 4, core: 2. Of those that a mesh axis runs over, the one named last changes fastest.
Arguments:
- inv_hessian: float32 [12288, 12288], P('row', 'col'), as said below
- weights: bfloat16 [24576, 12288], P('row', 'col'), may hold values from -6 to 6
- calib: bfloat16 [128, 12288], replicated, may hold values from -6 to 6
- block: int32 [1], replicated, may hold values from 0 to 47
Outputs:
- updated: float32 [12288, 12288], P('row', 'col')
- pruned: bfloat16 [24576, 12288], P('row', 'col')
Inputs may be any that keep to these rules, and one draw needn't show every extreme that they name: `inv_hessian`: symmetric and positive definite.
All inputs are finite; a program needn't handle non-finite values.
Results may differ from a plain program's by a relative error of at most 0.002.
Values may be sent and summed in bfloat16 or wider, within the bound.
A program may use at most 128 MiB of HBM per device.

v0:
```python
import jax
import jax.numpy as jnp
from jax import lax
from jax.sharding import PartitionSpec as P

B = 256


def spread(x, axis, root):
    mine = lax.axis_index(axis) == root
    return lax.psum(jnp.where(mine, x, jnp.zeros_like(x)), axis)


def per_device(inv_hessian, weights, calib, block):
    highest = lax.Precision.HIGHEST
    tile_rows, tile_cols = inv_hessian.shape
    row_index = lax.axis_index("row")
    col_index = lax.axis_index("col")
    calib_rows = lax.dynamic_slice_in_dim(calib, row_index * tile_rows, tile_rows, 1).astype(
        jnp.float32
    )
    calib_cols = lax.dynamic_slice_in_dim(calib, col_index * tile_cols, tile_cols, 1).astype(
        jnp.float32
    )
    left_part = jnp.dot(calib_rows, inv_hessian, precision=highest)
    left_cols = lax.psum(left_part, "row")
    right_part = jnp.dot(inv_hessian, calib_cols.T, precision=highest)
    inner_part = jnp.dot(left_cols, calib_cols.T, precision=highest)
    right_rows, inner = lax.psum((right_part, inner_part), "col")
    inner = jnp.eye(inner.shape[0], dtype=jnp.float32) + inner
    inner = 0.5 * (inner + inner.T)
    factor = jnp.linalg.cholesky(inner)
    solved = jax.scipy.linalg.cho_solve((factor, True), left_cols)
    updated = inv_hessian - jnp.dot(right_rows, solved, precision=highest)
    start = block[0] * B
    owner_row = start // tile_rows
    owner_col = start // tile_cols
    offset_row = start - owner_row * tile_rows
    offset_col = start - owner_col * tile_cols
    mine_rows = lax.dynamic_slice_in_dim(updated, offset_row, B, 0)
    strip = spread(mine_rows, "row", owner_row)
    mine_square = lax.dynamic_slice_in_dim(strip, offset_col, B, 1)
    square = spread(mine_square, "col", owner_col)
    mine_window = lax.dynamic_slice_in_dim(weights, offset_col, B, 1)
    window = spread(mine_window, "col", owner_col)
    square = 0.5 * (square + square.T)
    square_factor = jnp.linalg.cholesky(square)
    comp = jax.scipy.linalg.cho_solve((square_factor, True), strip).astype(jnp.bfloat16)
    product = jnp.dot(window, comp, preferred_element_type=jnp.float32)
    pruned = (weights.astype(jnp.float32) - product).astype(jnp.bfloat16)
    return (updated, pruned)


def solution(mesh):
    return jax.shard_map(
        per_device,
        mesh=mesh,
        in_specs=(P("row", "col"), P("row", "col"), P(), P()),
        out_specs=(P("row", "col"), P("row", "col")),
        check_vma=False,
    )
```

profile of v0, /device:TPU:0, one launch (start us, length us, event | category | flops | bytes accessed | tf_op | source)
XLA Modules:
  0.0 409.4 jit_solution(1854224920147407586)
XLA Ops:
  7.2 0.0 all-reduce.8.cloned.1.call-start
  7.2 1.8 copy-done
  9.1 11.5 %fusion.5 = f32[128,1536]{1,0:T(8,128)} fusion(f32[3072,1536]{1,0:T(8,128)} %param.4, bf16[128,12288]{1,0:T(8,128)(2,1)S(1)} %copy-done, s32[]{:T(128)S(6)} %select_n.54), kind=kOutput, calls=%fused_computation.16 | convolution fusion | flops 7247757312 | bytes 20447236 | tf_op jit(solution)/shard_map/dot_general | solution.py:25
  20.5 0.0 all-reduce.8.cloned.1.call-update
  20.6 0.0 all-reduce.16.cloned.1.call-start
  20.6 15.4 %convolution_bitcast_fusion = f32[3072,128]{0,1:T(8,128)} fusion(f32[3072,1536]{1,0:T(8,128)} %param.4, bf16[128,12288]{1,0:T(8,128)(2,1)S(1)} %copy-done, s32[]{:T(128)S(6)} %select_n.53), kind=kOutput, calls=%fused_computation.4 | convolution fusion | flops 7247757312 | bytes 20840452 | tf_op jit(solution)/shard_map/dot_general | solution.py:27
  36.0 36.1 %all-reduce.8.cloned.1.call-done = f32[128,1536]{1,0:T(8,128)} async-done(((f32[128,1536]{1,0:T(8,128)}), f32[128,1536]{1,0:T(8,128)}) %all-reduce.8.cloned.1.call-update) | async-done | bytes 786448 | tf_op jit(solution)/shard_map/psum | solution.py:26
  72.1 2.3 fusion.7
  74.4 0.0 all-reduce.16.cloned.1.call-update
  74.4 0.2 all-reduce.12.cloned.1.call-start
  75.3 18.7 %copy.8 = f32[3072,1536]{0,1:T(8,128)} copy(f32[3072,1536]{1,0:T(8,128)} %param.4) | data formatting | bytes 37748736 | tf_op args[0]
  94.1 43.7 %all-reduce.16.cloned.1.call-done = (f32[3072,128]{0,1:T(8,128)}, f32[128,128]{1,0:T(8,128)}) async-done(((f32[3072,128]{0,1:T(8,128)}, f32[128,128]{1,0:T(8,128)}), (f32[3072,128]{0,1:T(8,128)}, f32[128,128]{1,0:T(8,128)})) %all-reduce.16.cloned.1.call-update) | async-done | bytes 1638416 | tf_op jit(solution)/shard_map/psum | solution.py:29
  137.8 1.0 convert_add_fusion
  138.8 0.1 copy.6
  138.9 0.9 fusion.21
  139.8 0.1 copy.7
  139.9 11.7 %cholesky.52 = f32[128,128]{1,0:T(8,128)S(1)} custom-call(f32[128,128]{1,0:T(8,128)S(1)} %fusion.20), custom_call_target="Cholesky" | custom-call | tf_op jit(solution)/shard_map/jit(cholesky)/cholesky | solution.py:32
  151.6 0.6 compare_reduce_fusion.2
  152.3 0.7 fusion.12
  152.9 9.8 %custom-call.28 = f32[1,128,128]{1,2,0:T(8,128)S(1)} custom-call(f32[1,128,128]{2,1,0:T(8,128)S(1)} %fusion.12), custom_call_target="InvertDiagBlocksLowerTriangular" | custom-call | tf_op jit(solution)/shard_map/jit(_cho_solve)/triangular_solve | solution.py:33
  162.7 0.8 fusion.18
  163.6 0.8 fusion.16
  164.4 19.4 %convolution_subtract_fusion = f32[3072,1536]{0,1:T(8,128)S(1)} fusion(f32[3072,1536]{0,1:T(8,128)} %copy.8, f32[3072,128]{0,1:T(8,128)S(1)} %copy-done.5, f32[128,1536]{1,0:T(8,128)S(1)} %fusion.16), kind=kOutput, calls=%fused_computation.3 | convolution fusion | flops 7252475904 | bytes 40108032 | tf_op jit(solution)/shard_map/dot_general | solution.py:34
  183.8 6.8 %copy-done.2 = f32[3072,1536]{0,1:T(8,128)} copy-done((f32[3072,1536]{0,1:T(8,128)}, f32[3072,1536]{0,1:T(8,128)S(1)}, u32[]{:S(2)}) %copy-start.2) | copy-done | bytes 18874392
  190.6 1.3 dynamic-slice_select_fusion.1
  192.0 0.0 all-reduce.12.cloned.1.call-update
  192.0 0.0 all-reduce.14.cloned.1.call-start
  192.1 60.3 %all-reduce.12.cloned.1.call-done = f32[256,1536]{0,1:T(8,128)} async-done(((f32[256,1536]{0,1:T(8,128)}), f32[256,1536]{0,1:T(8,128)}) %all-reduce.12.cloned.1.call-update) | async-done | bytes 1572880 | tf_op jit(solution)/shard_map/psum | solution.py:11
  252.4 1.7 dynamic-slice_select_fusion.2
  254.1 0.0 all-reduce.14.cloned.1.call-update
  254.1 0.0 all-reduce.10.cloned.1.call-start
  254.1 4.2 %dynamic-slice_select_fusion = bf16[6144,256]{1,0:T(8,128)(2,1)} fusion(bf16[6144,1536]{1,0:T(8,128)(2,1)} %param.5, s32[]{:T(128)S(6)} %select_n.58, pred[]{:T(512)S(6)} %eq.8), kind=kLoop, calls=%fused_computation.5 | loop fusion | flops 1572864 | bytes 6291461 | tf_op jit(solution)/shard_map/jit(_where)/select_n | solution.py:11
  258.3 0.0 all-reduce.10.cloned.1.call-update
  258.3 18.9 %copy.16 = f32[3072,1536]{1,0:T(8,128)} copy(f32[3072,1536]{0,1:T(8,128)} %copy-done.2) | data formatting | bytes 37748736
  277.3 32.2 %all-reduce.14.cloned.1.call-done = f32[256,256]{0,1:T(8,128)} async-done(((f32[256,256]{0,1:T(8,128)}), f32[256,256]{0,1:T(8,128)}) %all-reduce.14.cloned.1.call-update) | async-done | bytes 262160 | tf_op jit(solution)/shard_map/psum | solution.py:11
  309.5 1.1 copy.10
  310.6 1.1 fusion.11
  311.7 0.1 copy.11
  311.9 11.7 %cholesky.104 = f32[128,128]{1,0:T(8,128)S(1)} custom-call(f32[128,128]{1,0:T(8,128)S(1)} %cholesky.129), custom_call_target="Cholesky" | custom-call | tf_op jit(solution)/shard_map/jit(cholesky)/cholesky | solution.py:47
  323.6 0.1 copy.12
  323.7 9.8 %custom-call.29 = f32[1,128,128]{1,2,0:T(8,128)S(1)} custom-call(f32[1,128,128]{2,1,0:T(8,128)S(1)} %get-tuple-element.29), custom_call_target="InvertDiagBlocksLowerTriangular" | custom-call | tf_op jit(solution)/shard_map/jit(cholesky)/cholesky | solution.py:47
  333.6 0.2 fusion.13
  333.8 0.3 convolution_subtract_fusion.3
  334.0 0.1 copy.13
  334.1 11.7 %cholesky.117 = f32[128,128]{1,0:T(8,128)S(1)} custom-call(f32[128,128]{1,0:T(8,128)S(1)} %convolution_subtract_fusion.3), custom_call_target="Cholesky" | custom-call | tf_op jit(solution)/shard_map/jit(cholesky)/cholesky | solution.py:47
  345.9 0.1 copy.14
  346.0 0.7 compare_reduce_fusion
  348.1 0.1 triangular_solve.123
  348.1 4.2 %while.1 = (s32[]{:T(128)}, f32[256,256]{0,1:T(8,128)S(1)}, s32[2,2]{1,0:T(2,128)S(1)}, f32[2,128,128]{2,1,0:T(8,128)S(1)}, s32[]{:T(128)}) while((s32[]{:T(128)}, f32[256,256]{0,1:T(8,128)S(1)}, s32[2,2]{1,0:T(2,128)S(1)}, f32[2,128,128]{2,1,0:T(8,128)S(1)}, s32[]{:T(128)}) %tuple.28), condition=%wide.while_cond, body=%wide.while_body.sunk | while | flops 2 | bytes 393329 | solution.py:48
  348.1 0.6 fusion.48
  348.7 1.4 dynamic-slice.7
  350.1 0.1 copy.20
  350.2 0.6 fusion.48
  350.8 1.4 dynamic-slice.7
  352.2 0.1 copy.20
  352.3 20.0 %custom-call.30 = f32[2,128,128]{1,2,0:T(8,128)S(1)} custom-call(f32[2,128,128]{2,1,0:T(8,128)S(1)} %get-tuple-element.9), custom_call_target="InvertDiagBlocksLowerTriangular" | custom-call | tf_op jit(solution)/shard_map/jit(_cho_solve)/triangular_solve | solution.py:48
  372.3 0.9 fusion
  373.2 2.5 convolution_subtract_fusion.2
  375.7 0.9 fusion.23
  376.6 1.6 fusion.31
  378.2 0.8 convolution_subtract_fusion.1
  378.9 0.8 convolution_convert_fusion
  379.7 8.4 %all-reduce.10.cloned.1.call-done = bf16[6144,256]{1,0:T(8,128)(2,1)} async-done(((bf16[6144,256]{1,0:T(8,128)(2,1)}), bf16[6144,256]{1,0:T(8,128)(2,1)}) %all-reduce.10.cloned.1.call-update) | async-done | bytes 3145744 | tf_op jit(solution)/shard_map/psum | solution.py:11
  388.1 14.3 %subtract_convert_fusion = bf16[6144,1536]{1,0:T(8,128)(2,1)} fusion(bf16[6144,1536]{1,0:T(8,128)(2,1)} %param.5, bf16[6144,256]{1,0:T(8,128)(2,1)} %all-reduce.10.cloned.1.call-done, bf16[128,1536]{1,0:T(8,128)(2,1)} %get-tuple-element.30, bf16[128,1536]{1,0:T(8,128)(2,1)S(1)} %convolution_convert_fusion), kind=kOutput, calls=%fused_computation.2 | convolution fusion | flops 4861722624 | bytes 41680896 | tf_op jit(solution)/shard_map/dot_general | solution.py:49
  (26 shorter events, 0.3 us)
Async XLA Ops:
  7.2 1.9 copy-start
  7.2 65.0 %all-reduce.8.cloned.1.call-start = ((), (), s32[]{:S(2)}) async-start(), calls=%async_computation | async-start | bytes 1572864 | tf_op jit(solution)/shard_map/psum | solution.py:26
  20.6 117.3 %all-reduce.16.cloned.1.call-start = ((), (), s32[]{:S(2)}) async-start(), calls=%async_computation.4 | async-start | bytes 3276800 | tf_op jit(solution)/shard_map/psum | solution.py:29
  74.4 178.0 %all-reduce.12.cloned.1.call-start = ((), (), s32[]{:S(2)}) async-start(), calls=%async_computation.2 | async-start | bytes 3145728 | tf_op jit(solution)/shard_map/psum | solution.py:11
  75.3 87.4 %copy-start.3 = (f32[128,1536]{1,0:T(8,128)S(1)}, f32[128,1536]{1,0:T(8,128)}, u32[]{:S(2)}) copy-start(f32[128,1536]{1,0:T(8,128)} %all-reduce.8.cloned.1.call-done) | copy-start | bytes 2359300
  137.8 26.6 %copy-start.5 = (f32[3072,128]{0,1:T(8,128)S(1)}, f32[3072,128]{0,1:T(8,128)}, u32[]{:S(2)}) copy-start(f32[3072,128]{0,1:T(8,128)} %get-tuple-element.24) | copy-start | bytes 4718596
  183.8 6.9 %copy-start.2 = (f32[3072,1536]{0,1:T(8,128)}, f32[3072,1536]{0,1:T(8,128)S(1)}, u32[]{:S(2)}) copy-start(f32[3072,1536]{0,1:T(8,128)S(1)} %convolution_subtract_fusion) | copy-start | bytes 56623108
  192.0 117.5 %all-reduce.14.cloned.1.call-start = ((), (), s32[]{:S(2)}) async-start(), calls=%async_computation.3 | async-start | bytes 524288 | tf_op jit(solution)/shard_map/psum | solution.py:11
  254.1 134.0 %all-reduce.10.cloned.1.call-start = ((), (), s32[]{:S(2)}) async-start(), calls=%async_computation.1 | async-start | bytes 6291456 | tf_op jit(solution)/shard_map/psum | solution.py:11
  310.6 61.7 %copy-start.4 = (f32[256,1536]{0,1:T(8,128)S(1)}, f32[256,1536]{0,1:T(8,128)}, u32[]{:S(2)}) copy-start(f32[256,1536]{0,1:T(8,128)} %all-reduce.12.cloned.1.call-done) | copy-start | bytes 4718596
  388.1 14.3 %copy-start.1 = (bf16[128,12288]{1,0:T(8,128)(2,1)S(1)}, bf16[128,12288]{1,0:T(8,128)(2,1)}, u32[]{:S(2)}) copy-start(bf16[128,12288]{1,0:T(8,128)(2,1)} %param.6) | copy-start | bytes 9437188
Sparse Core Ops, SparseCore 0:
  20.7 51.4 all-reduce.7
  75.3 62.4 all-reduce.15
  192.1 60.2 all-reduce.11
  254.6 54.8 all-reduce.13
  311.8 76.2 all-reduce.9
where the time goes:
time: 417 us; the launch traced here: 409 us
  waiting for transfers between devices  181 us (43%)
  other arithmetic  87 us (21%)
  matrix products  72.3 us (17%)
  local copies, waits for them, and re-layouts  52.3 us (13%)
  between operations  16.6 us (4%)
    psum x3, waiting for transfers between devices, spread(): return lax.psum(jnp.where(mine, x, jnp.zeros_like(x)), axis)  101 us
    unnamed x14, local copies, waits for them, and re-layouts  46.4 us
    psum x1, waiting for transfers between devices, per_device(): right_rows, inner = lax.psum((right_part, inner_part), 'col')  43.7 us
    psum x1, waiting for transfers between devices, per_device(): left_cols = lax.psum(left_part, 'row')  36.1 us
    another operation x6, other arithmetic, per_device(): square_factor = jnp.linalg.cholesky(square)  34 us
    another operation x3, other arithmetic, per_device(): jax.scipy.linalg.cho_solve((square_factor, True), strip)  20 us
    dot_general x1, matrix products, per_device(): updated = inv_hessian - jnp.dot(right_rows, solved, precision=highest)  19.4 us
    dot_general x1, matrix products, per_device(): right_part = jnp.dot(inv_hessian, calib_cols.T, precision=highest)  15.4 us
  transfers between devices with their start and end apart: 5, of which 5 were waited for; matrix products, arithmetic and copies ran while one was open for 31% of the time, Pallas kernels for 0%

commit v1 on v0

v1 whole, which is shorter than its diff:
```python
import functools

import jax
import jax.numpy as jnp
from jax import lax
from jax.experimental import pallas as pl
from jax.experimental.pallas import tpu as pltpu
from jax.sharding import PartitionSpec as P

B = 256
NB = 128
HIGH = lax.Precision.HIGHEST
VMEM_LIMIT = 48 * 1024 * 1024


def params(*semantics):
    return pltpu.CompilerParams(
        dimension_semantics=semantics or None, vmem_limit_bytes=VMEM_LIMIT
    )


def dot(a, b):
    return jnp.dot(a, b, precision=HIGH, preferred_element_type=jnp.float32)


def dot_t(a, b):
    return lax.dot_general(
        a, b, (((1,), (1,)), ((), ())), precision=HIGH, preferred_element_type=jnp.float32
    )


def bf_dot(a, b):
    return jnp.dot(a, b, preferred_element_type=jnp.float32)


def split2(x):
    hi = x.astype(jnp.bfloat16)
    lo = (x - hi.astype(jnp.float32)).astype(jnp.bfloat16)
    return hi, lo


def split3(x):
    hi = x.astype(jnp.bfloat16)
    rest = x - hi.astype(jnp.float32)
    mid = rest.astype(jnp.bfloat16)
    return hi, mid, (rest - mid.astype(jnp.float32)).astype(jnp.bfloat16)


def tile_of(n, most):
    t = most
    while n % t:
        t //= 2
    return t


def left_kernel(calib_ref, h_ref, out_ref):
    @pl.when(pl.program_id(0) == 0)
    def _():
        out_ref[...] = jnp.zeros_like(out_ref)

    c = calib_ref[...]
    hi, mid, lo = split3(h_ref[...])
    out_ref[...] += bf_dot(c, hi) + (bf_dot(c, mid) + bf_dot(c, lo))


def left_call(calib_rows, h):
    cal = calib_rows.shape[0]
    rows, cols = h.shape
    t = tile_of(rows, 512)
    return pl.pallas_call(
        left_kernel,
        grid=(rows // t,),
        in_specs=[
            pl.BlockSpec((cal, t), lambda i: (0, i)),
            pl.BlockSpec((t, cols), lambda i: (i, 0)),
        ],
        out_specs=pl.BlockSpec((cal, cols), lambda i: (0, 0)),
        out_shape=jax.ShapeDtypeStruct((cal, cols), jnp.float32),
        compiler_params=params("arbitrary"),
        cost_estimate=pl.CostEstimate(
            flops=6 * cal * rows * cols, bytes_accessed=4 * rows * cols, transcendentals=0
        ),
        name="left_part",
    )(calib_rows, h)


def inverses(mats):
    n = NB
    ri = lax.broadcasted_iota(jnp.int32, (n, n), 0)
    ci = lax.broadcasted_iota(jnp.int32, (n, n), 1)
    scales, ms = [], []
    for m in mats:
        only = jnp.where(ri == ci, m, 0.0)
        s_row = lax.rsqrt(jnp.sum(only, axis=0, keepdims=True))
        s_col = lax.rsqrt(jnp.sum(only, axis=1, keepdims=True))
        scales.append((s_row, s_col))
        ms.append(m * s_row * s_col)
    rk = lax.broadcasted_iota(jnp.int32, (n, 1), 0)
    ck = lax.broadcasted_iota(jnp.int32, (1, n), 1)
    for k in range(n):
        for i, m in enumerate(ms):
            row = m[k : k + 1, :]
            col = m[:, k : k + 1]
            inv = 1.0 / m[k : k + 1, k : k + 1]
            row = (row + jnp.where(ck == k, 1.0, 0.0)) * inv
            col = col - jnp.where(rk == k, 1.0, 0.0)
            ms[i] = m - col * row
    return [m * a * b for m, (a, b) in zip(ms, scales)]


def block_inverse_kernel(a_ref, out_ref):
    n = NB
    a = a_ref[...]
    a = 0.5 * (a + a.T)
    a11, a21, a22 = a[:n, :n], a[n:, :n], a[n:, n:]
    (p,) = inverses([a11])
    p = 0.5 * (p + p.T)
    w = dot(a21, p)
    (q,) = inverses([a22 - dot_t(w, a21)])
    q = 0.5 * (q + q.T)
    off = -dot(q, w)
    out_ref[:n, :n] = p - dot(w.T, off)
    out_ref[n:, :n] = off
    out_ref[:n, n:] = off.T
    out_ref[n:, n:] = q


def block_inverse(a):
    return pl.pallas_call(
        block_inverse_kernel,
        out_shape=jax.ShapeDtypeStruct(a.shape, jnp.float32),
        compiler_params=params(),
        name="block_inverse",
    )(a)


def small_kernel(inner_ref, lmt_ref, ainv_ref, inv_ref, x_ref, sinv_ref):
    inner = inner_ref[...]
    ri = lax.broadcasted_iota(jnp.int32, inner.shape, 0)
    ci = lax.broadcasted_iota(jnp.int32, inner.shape, 1)
    inner = jnp.where(ri == ci, 1.0, 0.0) + 0.5 * (inner + inner.T)
    lmt = lmt_ref[...]
    x = dot(ainv_ref[...], lmt)
    s = inner - dot(lmt.T, x)
    s = 0.5 * (s + s.T)
    a, b = inverses([inner, s])
    inv_ref[...] = 0.5 * (a + a.T)
    sinv_ref[...] = 0.5 * (b + b.T)
    x_ref[...] = x


def small(inner, lmt, ainv):
    f = jnp.float32
    return pl.pallas_call(
        small_kernel,
        out_shape=(
            jax.ShapeDtypeStruct(inner.shape, f),
            jax.ShapeDtypeStruct(lmt.shape, f),
            jax.ShapeDtypeStruct(inner.shape, f),
        ),
        compiler_params=params(),
        name="small_inverses",
    )(inner, lmt, ainv)


def comp_kernel(hm_ref, left_ref, lmt_ref, ainv_ref, x_ref, sinv_ref, out_ref):
    t = dot(ainv_ref[...], hm_ref[...])
    lm = lmt_ref[...].T
    v = dot(sinv_ref[...], left_ref[...] - dot(lm, t))
    out_ref[...] = (t - dot(x_ref[...], v)).astype(jnp.bfloat16)


def comp_call(hm, left, lmt, ainv, x, sinv):
    cols = hm.shape[1]
    t = tile_of(cols, 512)
    whole = lambda a: pl.BlockSpec(a.shape, lambda i: (0, 0))
    wide = lambda a: pl.BlockSpec((a.shape[0], t), lambda i: (0, i))
    return pl.pallas_call(
        comp_kernel,
        grid=(cols // t,),
        in_specs=[wide(hm), wide(left), whole(lmt), whole(ainv), whole(x), whole(sinv)],
        out_specs=pl.BlockSpec((hm.shape[0], t), lambda i: (0, i)),
        out_shape=jax.ShapeDtypeStruct(hm.shape, jnp.bfloat16),
        compiler_params=params("arbitrary"),
        name="comp",
    )(hm, left, lmt, ainv, x, sinv)


def update_kernel(right_ref, inv_ref, left_ref, h_ref, out_ref, s_ref):
    cal = left_ref.shape[0]

    @pl.when(pl.program_id(0) == 0)
    def _():
        hi, lo = split2(dot(inv_ref[...], left_ref[...]))
        s_ref[0:cal] = hi
        s_ref[cal : 2 * cal] = lo
        s_ref[2 * cal : 3 * cal] = hi

    hi, lo = split2(right_ref[...].T)
    r = jnp.concatenate([hi, hi, lo], axis=1)
    out_ref[...] = h_ref[...] - bf_dot(r, s_ref[...])


def update_call(right, inv, left, h):
    cal = left.shape[0]
    rows, cols = h.shape
    t = tile_of(rows, 512)
    return pl.pallas_call(
        update_kernel,
        grid=(rows // t,),
        in_specs=[
            pl.BlockSpec((cal, t), lambda i: (0, i)),
            pl.BlockSpec(inv.shape, lambda i: (0, 0)),
            pl.BlockSpec(left.shape, lambda i: (0, 0)),
            pl.BlockSpec((t, cols), lambda i: (i, 0)),
        ],
        out_specs=pl.BlockSpec((t, cols), lambda i: (i, 0)),
        out_shape=jax.ShapeDtypeStruct(h.shape, jnp.float32),
        scratch_shapes=[pltpu.VMEM((3 * cal, cols), jnp.bfloat16)],
        compiler_params=params("arbitrary"),
        cost_estimate=pl.CostEstimate(
            flops=6 * cal * rows * cols, bytes_accessed=8 * rows * cols, transcendentals=0
        ),
        name="update",
    )(right, inv, left, h)


def prune_kernel(window_ref, comp_ref, w_ref, out_ref):
    product = bf_dot(window_ref[...], comp_ref[...])
    out_ref[...] = (w_ref[...].astype(jnp.float32) - product).astype(jnp.bfloat16)


def prune_call(window, comp, w):
    rows, cols = w.shape
    t = tile_of(rows, 768)
    return pl.pallas_call(
        prune_kernel,
        grid=(rows // t,),
        in_specs=[
            pl.BlockSpec((t, window.shape[1]), lambda i: (i, 0)),
            pl.BlockSpec(comp.shape, lambda i: (0, 0)),
            pl.BlockSpec((t, cols), lambda i: (i, 0)),
        ],
        out_specs=pl.BlockSpec((t, cols), lambda i: (i, 0)),
        out_shape=jax.ShapeDtypeStruct(w.shape, jnp.bfloat16),
        compiler_params=params("arbitrary"),
        cost_estimate=pl.CostEstimate(
            flops=2 * rows * cols * window.shape[1],
            bytes_accessed=4 * rows * cols,
            transcendentals=0,
        ),
        name="prune",
    )(window, comp, w)


def per_device(h, w, calib, block):
    rows, cols = h.shape
    r = lax.axis_index("row")
    c = lax.axis_index("col")
    start = block[0] * B
    owner_row, owner_col = start // rows, start // cols
    mine_row, mine_col = r == owner_row, c == owner_col
    off_row, off_col = start - owner_row * rows, start - owner_col * cols

    win = lax.dynamic_slice_in_dim(w, off_col, B, 1)
    window = lax.psum(jnp.where(mine_col, win, jnp.zeros_like(win)), "col")

    strip = lax.dynamic_slice_in_dim(h, off_row, B, 0)
    strip = jnp.where(mine_row, strip, 0.0)
    square = lax.dynamic_slice_in_dim(strip, off_col, B, 1)
    square = lax.psum(jnp.where(mine_col, square, 0.0), ("row", "col"))

    calib_rows = lax.dynamic_slice_in_dim(calib, r * rows, rows, 1)
    calib_cols = lax.dynamic_slice_in_dim(calib, c * cols, cols, 1).astype(jnp.float32)
    part = left_call(calib_rows, h)
    both = dot_t(jnp.concatenate([part, strip], axis=0), calib_cols)
    both = lax.psum(both, ("row", "col"))
    cal = part.shape[0]
    inner, lmt = both[:cal], both[cal:]
    left = lax.psum(part, "row")
    hm = lax.psum(strip, "row")

    n = rows // cols
    zero = jnp.zeros_like(left)
    right = jnp.concatenate(
        [jnp.where(c == r * n + j, left, zero) for j in range(n)], axis=1
    )
    right = lax.psum(right, "col")

    ainv = block_inverse(square)
    inv, x, sinv = small(inner, lmt, ainv)
    updated = update_call(right, inv, left, h)
    comp = comp_call(hm, left, lmt, ainv, x, sinv)
    pruned = prune_call(window, comp, w)
    return (updated, pruned)


def solution(mesh):
    return jax.shard_map(
        per_device,
        mesh=mesh,
        in_specs=(P("row", "col"), P("row", "col"), P(), P()),
        out_specs=(P("row", "col"), P("row", "col")),
        check_vma=False,
    )
```

time: 417 us -> 416 us (level); the launches traced: 409 us -> 415 us
  waiting for transfers between devices: 181 us -> 287 us
  Pallas kernels: 0 us -> 85.8 us
  other arithmetic: 87 us -> 11 us
  matrix products: 72.3 us -> 3.45 us
  local copies, waits for them, and re-layouts: 52.3 us -> 12.6 us
    psum x5 -> x4, waiting for transfers between devices: 181 us -> 286 us  [the longest x1 130 us: per_device(): both = lax.psum(both, ('row', 'col'))]
    pallas_call x0 -> x6, Pallas kernels: none -> 85.8 us  [the longest x1 23 us: block_inverse(): pl.pallas_call(block_inverse_kernel, out_shape=jax.ShapeDtypeStruct(a.sha...]
    another operation x14 -> x0, other arithmetic: 76.9 us -> none  [the longest x6 34 us: per_device(): square_factor = jnp.linalg.cholesky(square)]
    dot_general x5 -> x1, matrix products: 62.8 us -> 3.45 us  [dot_t(): lax.dot_general(a, b, (((1,), (1,)), ((), ())), precision=HIGH, preferred...]
    unnamed x14 -> x22, local copies, waits for them, and re-layouts: 46.4 us -> 10.8 us
    another operation x10 -> x0, matrix products: 9.48 us -> none  [the longest x6 7.39 us: per_device(): jax.scipy.linalg.cho_solve((square_factor, True), strip)]
    another operation x18 -> x0, local copies, waits for them, and re-layouts: 4.51 us -> none
    select_n x3 -> x4, other arithmetic: 7.17 us -> 9.73 us  [the longest x1 4.11 us: per_device(): window = lax.psum(jnp.where(mine_col, win, jnp.zeros_like(win)), 'col')]
  transfers between devices with their start and end apart: 5 -> 4, of which waited for: 5 -> 4; matrix products, arithmetic and copies ran while one was open for 31% -> 2% of each run, Pallas kernels for 0% -> 14%
where the time goes in v1:
time: 416 us; the launch traced here: 415 us
  waiting for transfers between devices  287 us (69%)
  Pallas kernels  85.8 us (21%)
  between operations  14.7 us (4%)
  local copies, waits for them, and re-layouts  12.6 us (3%)
  other arithmetic  11 us (3%)
    psum x1, waiting for transfers between devices, per_device(): both = lax.psum(both, ('row', 'col'))  130 us
    psum x1, waiting for transfers between devices, per_device(): left = lax.psum(part, 'row')  75.6 us
    psum x1, waiting for transfers between devices, per_device(): right = lax.psum(right, 'col')  44.6 us
    psum x1, waiting for transfers between devices, per_device(): window = lax.psum(jnp.where(mine_col, win, jnp.zeros_like(win)), 'col')  35.2 us
    pallas_call x1, Pallas kernels, block_inverse(): pl.pallas_call(block_inverse_kernel, out_shape=jax.ShapeDtypeStruct(a.sha...  23 us
    pallas_call x1, Pallas kernels, prune_call(): pl.pallas_call(prune_kernel, grid=(rows // t,), in_specs=[pl.BlockSpec((t...  17.1 us
    pallas_call x1, Pallas kernels, update_call(): pl.pallas_call(update_kernel, grid=(rows // t,), in_specs=[pl.BlockSpec((...  17 us
    pallas_call x1, Pallas kernels, small(): pl.pallas_call(small_kernel, out_shape=(jax.ShapeDtypeStruct(inner.shape,...  11.7 us
  transfers between devices with their start and end apart: 4, of which 4 were waited for; matrix products, arithmetic and copies ran while one was open for 2% of the time, Pallas kernels for 14%

profile of v1, /device:TPU:0, one launch (start us, length us, event | category | flops | bytes accessed | tf_op | source)
XLA Modules:
  0.0 414.8 jit_solution(3623921362625217943)
XLA Ops:
  7.2 0.0 copy-start
  8.0 1.0 copy-done
  9.1 0.1 constant_dynamic-slice_fusion.calib_ref
  9.1 11.1 %left_part.1 = f32[128,1536]{1,0:T(8,128)S(1)} custom-call(bf16[128,3072]{1,0:T(8,128)(2,1)S(1)} %constant_dynamic-slice_fusion.calib_ref, f32[3072,1536]{1,0:T(8,128)} %h_ref.3), custom_call_target="tpu_custom_call" | custom-call | flops 3623878656 | bytes 18874368 | tf_op jit(solution)/shard_map/left_part/pallas_call | solution.py:70
  20.2 0.0 copy-start.2
  20.2 0.9 copy-done.2
  21.1 2.7 dynamic-slice_select_fusion.1
  23.8 3.4 fusion
  27.2 1.7 dynamic-slice_select_fusion.2
  28.9 0.0 all-reduce.13.cloned.1.call-start
  28.9 0.7 all-reduce.13.cloned.1.call-update
  29.6 0.0 all-reduce.11.cloned.1.call-start
  29.6 0.7 all-reduce.11.cloned.1.call-update
  30.4 0.0 all-reduce.9.cloned.1.call-start
  30.4 4.1 dynamic-slice_select_fusion
  34.5 0.0 all-reduce.9.cloned.1.call-update
  34.5 0.2 all-reduce.7.cloned.1.call-start
  34.8 75.6 %all-reduce.13.cloned.1.call-done = (f32[128,1536]{1,0:T(8,128)}, f32[256,1536]{1,0:T(8,128)}) async-done(((f32[128,1536]{1,0:T(8,128)}, f32[256,1536]{1,0:T(8,128)}), (f32[128,1536]{1,0:T(8,128)}, f32[256,1536]{1,0:T(8,128)})) %all-reduce.13.cloned.1.call-update) | async-done | bytes 2359312 | tf_op jit(solution)/shard_map/psum | solution.py:280
  110.4 1.3 broadcast_select_fusion.1
  111.7 0.0 copy-start.3
  111.7 1.3 pad_maximum_fusion
  113.0 0.0 all-reduce.7.cloned.1.call-update
  113.0 130.1 %all-reduce.11.cloned.1.call-done = (f32[384,128]{1,0:T(8,128)}, f32[256,256]{1,0:T(8,128)}) async-done(((f32[384,128]{1,0:T(8,128)}, f32[256,256]{1,0:T(8,128)}), (f32[384,128]{1,0:T(8,128)}, f32[256,256]{1,0:T(8,128)})) %all-reduce.11.cloned.1.call-update) | async-done | bytes 458768 | tf_op jit(solution)/shard_map/psum | solution.py:277
  243.1 0.8 slice.8.inner_ref
  244.0 0.9 slice.9.lmt_ref
  244.9 0.0 copy-start.10
  244.9 0.9 copy-done.10
  245.8 23.0 %block_inverse.1.ainv_ref = f32[256,256]{1,0:T(8,128)S(1)} custom-call(f32[256,256]{1,0:T(8,128)S(1)} %copy-done.10), custom_call_target="tpu_custom_call" | custom-call | tf_op jit(solution)/shard_map/block_inverse/pallas_call | solution.py:129
  268.9 11.7 %small_inverses.1 = (f32[128,128]{1,0:T(8,128)S(1)}, f32[256,128]{1,0:T(8,128)S(1)}, f32[128,128]{1,0:T(8,128)S(1)}) custom-call(f32[128,128]{1,0:T(8,128)S(1)} %slice.8.inner_ref, f32[256,128]{1,0:T(8,128)S(1)} %slice.9.lmt_ref, f32[256,256]{1,0:T(8,128)S(1)} %block_inverse.1.ainv_ref), custom_call_target="tpu_custom_call" | custom-call | tf_op jit(solution)/shard_map/small_inverses/pallas_call | solution.py:154
  280.6 0.0 copy-done.3
  280.6 0.0 copy-start.9
  280.6 1.4 copy-done.9
  282.0 5.9 %comp.1.comp_ref = bf16[256,1536]{1,0:T(8,128)(2,1)S(1)} custom-call(f32[256,1536]{1,0:T(8,128)S(1)} %copy-done.9, f32[128,1536]{1,0:T(8,128)S(1)} %copy-done.3, f32[256,128]{1,0:T(8,128)S(1)} %slice.9.lmt_ref, f32[256,256]{1,0:T(8,128)S(1)} %block_inverse.1.ainv_ref, f32[256,128]{1,0:T(8,128)S(1)} %get-tuple-element.6.x_ref, ...), custom_call_target="tpu_custom_call" | custom-call | tf_op jit(solution)/shard_map/comp/pallas_call | solution.py:178
  287.9 0.0 copy-start.6
  287.9 0.9 copy-done.6
  288.8 35.2 %all-reduce.9.cloned.1.call-done.window_ref = bf16[6144,256]{1,0:T(8,128)(2,1)} async-done(((bf16[6144,256]{1,0:T(8,128)(2,1)}), bf16[6144,256]{1,0:T(8,128)(2,1)}) %all-reduce.9.cloned.1.call-update) | async-done | bytes 3145744 | tf_op jit(solution)/shard_map/psum | solution.py:266
  324.0 0.0 copy-start.5
  324.0 1.9 copy-done.5
  325.9 0.0 copy-start.7
  325.9 1.1 copy-done.7
  327.0 17.1 %prune.1 = bf16[6144,1536]{1,0:T(8,128)(2,1)} custom-call(bf16[6144,256]{1,0:T(8,128)(2,1)S(1)} %copy-done.5, bf16[256,1536]{1,0:T(8,128)(2,1)S(1)} %copy-done.7, bf16[6144,1536]{1,0:T(8,128)(2,1)} %w_ref.1), custom_call_target="tpu_custom_call" | custom-call | flops 4831838208 | bytes 37748736 | tf_op jit(solution)/shard_map/prune/pallas_call | solution.py:236
  344.2 44.6 %all-reduce.7.cloned.1.call-done.right_ref = f32[128,3072]{1,0:T(8,128)} async-done(((f32[128,3072]{1,0:T(8,128)}), f32[128,3072]{1,0:T(8,128)}) %all-reduce.7.cloned.1.call-update) | async-done | bytes 1572880 | tf_op jit(solution)/shard_map/psum | solution.py:288
  388.7 0.0 copy-start.4
  388.7 1.1 copy-done.4
  389.9 0.0 copy-start.8
  389.9 1.4 copy-done.8
  391.3 0.0 copy-start.1
  391.3 17.0 %update.1 = f32[3072,1536]{1,0:T(8,128)} custom-call(f32[128,3072]{1,0:T(8,128)S(1)} %copy-done.8, f32[128,128]{1,0:T(8,128)S(1)} %get-tuple-element.5.inv_ref, f32[128,1536]{1,0:T(8,128)S(1)} %copy-done.4, f32[3072,1536]{1,0:T(8,128)} %h_ref.3), custom_call_target="tpu_custom_call" | custom-call | flops 3623878656 | bytes 37748736 | tf_op jit(solution)/shard_map/update/pallas_call | solution.py:208
  408.3 0.0 copy-done.1
Async XLA Ops:
  7.2 1.9 copy-start
  20.2 0.9 copy-start.2
  28.9 81.5 %all-reduce.13.cloned.1.call-start = ((), (), s32[]{:S(2)}) async-start(), calls=%async_computation.3 | async-start | bytes 4718592 | tf_op jit(solution)/shard_map/psum | solution.py:280
  29.6 213.5 %all-reduce.11.cloned.1.call-start = ((), (), s32[]{:S(2)}) async-start(), calls=%async_computation.2 | async-start | bytes 917504 | tf_op jit(solution)/shard_map/psum | solution.py:277
  30.4 293.6 %all-reduce.9.cloned.1.call-start = ((), (), s32[]{:S(2)}) async-start(), calls=%async_computation.1 | async-start | bytes 6291456 | tf_op jit(solution)/shard_map/psum | solution.py:266
  34.5 354.2 %all-reduce.7.cloned.1.call-start = ((), (), s32[]{:S(2)}) async-start(), calls=%async_computation | async-start | bytes 3145728 | tf_op jit(solution)/shard_map/psum | solution.py:288
  111.7 168.8 %copy-start.3 = (f32[128,1536]{1,0:T(8,128)S(1)}, f32[128,1536]{1,0:T(8,128)}, u32[]{:S(2)}) copy-start(f32[128,1536]{1,0:T(8,128)} %get-tuple-element.10.left_ref) | copy-start | bytes 2359300
  244.9 1.0 copy-start.10
  280.6 1.4 copy-start.9
  287.9 0.9 copy-start.6
  324.0 1.9 copy-start.5
  325.9 1.1 copy-start.7
  388.7 1.1 copy-start.4
  389.9 1.4 copy-start.8
  391.3 17.0 %copy-start.1 = (bf16[128,12288]{1,0:T(8,128)(2,1)S(1)}, bf16[128,12288]{1,0:T(8,128)(2,1)}, u32[]{:S(2)}) copy-start(bf16[128,12288]{1,0:T(8,128)(2,1)} %param.6) | copy-start | bytes 9437188
Sparse Core Ops, SparseCore 0:
  33.4 76.9 all-reduce.12
  116.7 126.4 all-reduce.10
  246.1 77.8 all-reduce.8
  326.8 61.8 all-reduce.6

commit v2 on v1

--- a/solution.py
+++ b/solution.py
@@ -186,6 +186,164 @@
     )(hm, left, lmt, ainv, x, sinv)
 
 
+def exchange_kernel(
+    nr, nc, n, g_ref, part_ref, gout, left, right, gbuf, gsum, gbuf2, lbuf,
+    g1s, g1r, g2s, g2r, g3s, g3r, l1s, l1r, l2s, l2r, cs, cr, ss, sr,
+):
+    r = lax.axis_index("row")
+    c = lax.axis_index("col")
+    grp, lane, ng = c // n, c % n, nc // n
+    ch = g_ref.shape[0] // nc
+    cal = part_ref.shape[0]
+    lc = cal // nr
+
+    def send(src, dst, s, v, axis, peer):
+        return pltpu.make_async_remote_copy(
+            src_ref=src, dst_ref=dst, send_sem=s, recv_sem=v,
+            device_id={axis: peer}, device_id_type=pl.DeviceIdType.MESH,
+        )
+
+    def row_peer(d):
+        return lax.rem(r + d, nr)
+
+    def col_peer(d):
+        return lax.rem(c + d, nc)
+
+    barrier = pltpu.get_barrier_semaphore()
+    for d in range(1, nr):
+        pl.semaphore_signal(
+            barrier, inc=1, device_id={"row": row_peer(d)}, device_id_type=pl.DeviceIdType.MESH
+        )
+    for d in range(1, nc):
+        pl.semaphore_signal(
+            barrier, inc=1, device_id={"col": col_peer(d)}, device_id_type=pl.DeviceIdType.MESH
+        )
+    pl.semaphore_wait(barrier, nr + nc - 2)
+
+    def part_rows(ref, i, size, base=0):
+        return ref.at[pl.ds(pl.multiple_of(base + i * size, 8), size)]
+
+    l1, l2, g1, g2, g3 = [], [], [], [], []
+    for d in range(1, nr):
+        p = row_peer(d)
+        l1.append(send(part_rows(part_ref, p, lc), lbuf.at[d], l1s.at[d], l1r.at[d], "row", p))
+        l1[-1].start()
+    for d in range(1, nc):
+        p = col_peer(d)
+        g1.append(send(part_rows(g_ref, p, ch), gbuf.at[d], g1s.at[d], g1r.at[d], "col", p))
+        g1[-1].start()
+
+    for x in g1:
+        x.wait_recv()
+    total = g_ref[pl.ds(pl.multiple_of(c * ch, 8), ch)]
+    for d in range(1, nc):
+        total += gbuf[d]
+    gsum[...] = total
+    for d in range(1, nr):
+        g2.append(send(gsum, gbuf2.at[d], g2s.at[d], g2r.at[d], "row", row_peer(d)))
+        g2[-1].start()
+
+    for x in l1:
+        x.wait_recv()
+    mine = pl.ds(pl.multiple_of(r * lc, 8), lc)
+    total = part_ref[mine]
+    for d in range(1, nr):
+        total += lbuf[d]
+    left[mine] = total
+    own = part_rows(left, r, lc)
+    for d in range(1, nr):
+        l2.append(send(own, own, l2s.at[d], l2r.at[d], "row", row_peer(d)))
+        l2[-1].start()
+
+    for x in g2:
+        x.wait_recv()
+    total = gsum[...]
+    for d in range(1, nr):
+        total += gbuf2[d]
+    gout[pl.ds(pl.multiple_of(c * ch, 8), ch)] = total
+    gown = part_rows(gout, c, ch)
+    for d in range(1, nc):
+        g3.append(send(gown, gown, g3s.at[d], g3r.at[d], "col", col_peer(d)))
+        g3[-1].start()
+
+    up, down = lax.rem(c + n, nc), lax.rem(c + nc - n, nc)
+    origin = grp == r
+    to_up = jnp.logical_and(grp >= r, grp + 1 < ng)
+    to_down = jnp.logical_and(grp <= r, grp > 0)
+
+    def sibling(e):
+        return grp * n + lax.rem(lane + e, n)
+
+    sends = []
+    for d in range(nr):
+        chunk = lax.rem(r + nr - d, nr)
+        src_left = part_rows(left, chunk, lc)
+        there = part_rows(right, chunk, lc, lane * cal)
+
+        if d > 0:
+            pl.when(origin)(l2[d - 1].wait_recv)
+
+        @pl.when(origin)
+        def _():
+            rows_in = pl.ds(pl.multiple_of(chunk * lc, 8), lc)
+            rows_out = pl.ds(pl.multiple_of(lane * cal + chunk * lc, 8), lc)
+            right[rows_out] = left[rows_in]
+
+        u = send(there, there, cs.at[0, d], cr.at[d], "col", up)
+        w = send(there, there, cs.at[1, d], cr.at[d], "col", down)
+        pl.when(jnp.logical_not(origin))(u.wait_recv)
+        pl.when(to_up)(u.start)
+        pl.when(to_down)(w.start)
+        sends += [(to_up, u), (to_down, w)]
+        for e in range(1, n):
+            x = send(there, there, ss.at[e, d], sr.at[e, d], "col", sibling(e))
+            x.start()
+            sends.append((None, x))
+
+    for x in l2:
+        pl.when(jnp.logical_not(origin))(x.wait_recv)
+    for x in g3:
+        x.wait_recv()
+    for pred, x in sends:
+        if pred is None:
+            x.wait()
+        else:
+            pl.when(pred)(x.wait_send)
+    for x in l1 + l2 + g1 + g2 + g3:
+        x.wait_send()
+
+
+def exchange(nr, nc, n, g, part):
+    f = jnp.float32
+    dma = lambda *shape: pltpu.SemaphoreType.DMA(shape)
+    cal, cols = part.shape
+    ch = g.shape[0] // nc
+    vmem = pl.BlockSpec(memory_space=pltpu.VMEM)
+    return pl.pallas_call(
+        functools.partial(exchange_kernel, nr, nc, n),
+        in_specs=[vmem, vmem],
+        out_specs=[vmem, vmem, vmem],
+        out_shape=(
+            jax.ShapeDtypeStruct(g.shape, f),
+            jax.ShapeDtypeStruct(part.shape, f),
+            jax.ShapeDtypeStruct((n * cal, cols), f),
+        ),
+        scratch_shapes=[
+            pltpu.VMEM((nc, ch, g.shape[1]), f),
+            pltpu.VMEM((ch, g.shape[1]), f),
+            pltpu.VMEM((nr, ch, g.shape[1]), f),
+            pltpu.VMEM((nr, cal // nr, cols), f),
+            dma(nc), dma(nc), dma(nr), dma(nr), dma(nc), dma(nc),
+            dma(nr), dma(nr), dma(nr), dma(nr),
+            dma(2, nr), dma(nr), dma(n, nr), dma(n, nr),
+        ],
+        compiler_params=pltpu.CompilerParams(
+            collective_id=0, has_side_effects=True, vmem_limit_bytes=VMEM_LIMIT
+        ),
+        name="exchange",
+    )(g, part)
+
+
 def update_kernel(right_ref, inv_ref, left_ref, h_ref, out_ref, s_ref):
     cal = left_ref.shape[0]
 
@@ -204,12 +362,13 @@
 def update_call(right, inv, left, h):
     cal = left.shape[0]
     rows, cols = h.shape
-    t = tile_of(rows, 512)
+    t = tile_of(cols, 512)
+    per = cols // t
     return pl.pallas_call(
         update_kernel,
         grid=(rows // t,),
         in_specs=[
-            pl.BlockSpec((cal, t), lambda i: (0, i)),
+            pl.BlockSpec((cal, t), lambda i: (i // per, i % per)),
             pl.BlockSpec(inv.shape, lambda i: (0, 0)),
             pl.BlockSpec(left.shape, lambda i: (0, 0)),
             pl.BlockSpec((t, cols), lambda i: (i, 0)),
@@ -268,29 +427,24 @@
     strip = lax.dynamic_slice_in_dim(h, off_row, B, 0)
     strip = jnp.where(mine_row, strip, 0.0)
     square = lax.dynamic_slice_in_dim(strip, off_col, B, 1)
-    square = lax.psum(jnp.where(mine_col, square, 0.0), ("row", "col"))
+    square = jnp.where(mine_col, square, 0.0)
 
     calib_rows = lax.dynamic_slice_in_dim(calib, r * rows, rows, 1)
     calib_cols = lax.dynamic_slice_in_dim(calib, c * cols, cols, 1).astype(jnp.float32)
     part = left_call(calib_rows, h)
+    cal = part.shape[0]
     both = dot_t(jnp.concatenate([part, strip], axis=0), calib_cols)
-    both = lax.psum(both, ("row", "col"))
-    cal = part.shape[0]
-    inner, lmt = both[:cal], both[cal:]
-    left = lax.psum(part, "row")
-    hm = lax.psum(strip, "row")
-
-    n = rows // cols
-    zero = jnp.zeros_like(left)
-    right = jnp.concatenate(
-        [jnp.where(c == r * n + j, left, zero) for j in range(n)], axis=1
-    )
-    right = lax.psum(right, "col")
+    g = jnp.concatenate([both, square[:, :NB], square[:, NB:]], axis=0)
+
+    g, left, right = exchange(lax.axis_size("row"), lax.axis_size("col"), rows // cols, g, part)
+    inner, lmt = g[:cal], g[cal : cal + B]
+    square = jnp.concatenate([g[cal + B : cal + 2 * B], g[cal + 2 * B :]], axis=1)
 
     ainv = block_inverse(square)
     inv, x, sinv = small(inner, lmt, ainv)
+    comp = comp_call(strip, left, lmt, ainv, x, sinv)
+    comp = lax.psum(jnp.where(mine_row, comp, jnp.zeros_like(comp)), "row")
     updated = update_call(right, inv, left, h)
-    comp = comp_call(hm, left, lmt, ainv, x, sinv)
     pruned = prune_call(window, comp, w)
     return (updated, pruned)
 

time: 416 us -> 283 us (0.68)
  waiting for transfers between devices: 287 us -> 119 us
  Pallas kernels: 85.8 us -> 130 us
  local copies, waits for them, and re-layouts: 12.6 us -> 8.06 us
    psum x3 -> x1, waiting for transfers between devices: 250 us -> 39.2 us  [per_device(): comp = lax.psum(jnp.where(mine_row, comp, jnp.zeros_like(comp)), 'row')]
    psum x1, waiting for transfers between devices: 35.2 us -> 80 us  [per_device(): window = lax.psum(jnp.where(mine_col, win, jnp.zeros_like(win)), 'col')]
    pallas_call x0 -> x1, Pallas kernels: none -> 44.1 us  [exchange(): pl.pallas_call(functools.partial(exchange_kernel, nr, nc, n), in_specs=[v...]
    unnamed x22 -> x24, local copies, waits for them, and re-layouts: 10.8 us -> 7.95 us
  transfers between devices with their start and end apart: 4 -> 2, of which waited for: 4 -> 2; matrix products, arithmetic and copies ran while one was open for 2% -> 1% of each run, Pallas kernels for 14% -> 6%
where the time goes in v2:
time: 283 us; the launch traced here: 282 us
  Pallas kernels  130 us (46%)
  waiting for transfers between devices  119 us (42%)
  between operations  15.1 us (5%)
  local copies, waits for them, and re-layouts  8.06 us (3%)
  other arithmetic  6.95 us (2%)
  matrix products  2.93 us (1%)
    psum x1, waiting for transfers between devices, per_device(): window = lax.psum(jnp.where(mine_col, win, jnp.zeros_like(win)), 'col')  80 us
    pallas_call x1, Pallas kernels, exchange(): pl.pallas_call(functools.partial(exchange_kernel, nr, nc, n), in_specs=[v...  44.1 us
    psum x1, waiting for transfers between devices, per_device(): comp = lax.psum(jnp.where(mine_row, comp, jnp.zeros_like(comp)), 'row')  39.2 us
    pallas_call x1, Pallas kernels, block_inverse(): pl.pallas_call(block_inverse_kernel, out_shape=jax.ShapeDtypeStruct(a.sha...  23 us
    pallas_call x1, Pallas kernels, prune_call(): pl.pallas_call(prune_kernel, grid=(rows // t,), in_specs=[pl.BlockSpec((t...  17.2 us
    pallas_call x1, Pallas kernels, update_call(): pl.pallas_call(update_kernel, grid=(rows // t,), in_specs=[pl.BlockSpec((...  16.9 us
    pallas_call x1, Pallas kernels, small(): pl.pallas_call(small_kernel, out_shape=(jax.ShapeDtypeStruct(inner.shape,...  11.7 us
    pallas_call x1, Pallas kernels, left_call(): pl.pallas_call(left_kernel, grid=(rows // t,), in_specs=[pl.BlockSpec((ca...  11.1 us
  transfers between devices with their start and end apart: 2, of which 2 were waited for; matrix products, arithmetic and copies ran while one was open for 1% of the time, Pallas kernels for 6%

profile of v2, /device:TPU:0, one launch (start us, length us, event | category | flops | bytes accessed | tf_op | source)
XLA Modules:
  0.0 282.3 jit_solution(6525499616184580620)
XLA Ops:
  7.2 0.0 copy-start
  7.2 0.0 all-reduce.5.cloned.1.call-start
  8.1 1.0 copy-done
  9.1 0.1 constant_dynamic-slice_fusion.calib_ref
  9.1 11.1 %left_part.1.part_ref = f32[128,1536]{1,0:T(8,128)S(1)} custom-call(bf16[128,3072]{1,0:T(8,128)(2,1)S(1)} %constant_dynamic-slice_fusion.calib_ref, f32[3072,1536]{1,0:T(8,128)} %h_ref.3), custom_call_target="tpu_custom_call" | custom-call | flops 3623878656 | bytes 18874368 | tf_op jit(solution)/shard_map/left_part/pallas_call | solution.py:70
  20.2 0.0 copy-start.4
  20.2 1.8 dynamic-slice_select_fusion.1.hm_ref
  22.0 0.0 copy-start.2
  22.0 1.1 copy-done.2
  23.2 0.0 copy-done.4
  23.2 0.0 copy-start.5
  23.2 0.0 copy-start.3
  23.3 2.9 %fusion = f32[384,128]{1,0:T(8,128)S(1)} fusion(f32[256,1536]{1,0:T(8,128)} %copy-done.2, f32[128,1536]{1,0:T(8,128)} %copy-done.4, bf16[128,12288]{1,0:T(8,128)(2,1)S(1)} %copy-done, s32[]{:T(128)S(6)} %select_n.56), kind=kOutput, calls=%fused_computation.1 | convolution fusion | flops 906559488 | bytes 2949124 | tf_op jit(solution)/shard_map/dot_general | solution.py:27
  26.2 0.0 copy-done.5
  26.2 44.1 %exchange.1 = (f32[896,128]{1,0:T(8,128)S(1)}, f32[128,1536]{1,0:T(8,128)S(1)}, f32[256,1536]{1,0:T(8,128)S(1)}) custom-call(f32[896,128]{1,0:T(8,128)S(1)} %pad_maximum_fusion.g_ref, f32[128,1536]{1,0:T(8,128)S(1)} %copy-done.5), custom_call_target="tpu_custom_call" | custom-call | tf_op jit(solution)/shard_map/exchange/pallas_call | solution.py:322
  70.3 0.0 copy-start.9
  70.3 1.1 copy-done.9
  71.5 0.0 copy-start.7
  71.5 23.0 %block_inverse.1.ainv_ref = f32[256,256]{1,0:T(8,128)S(1)} custom-call(f32[256,256]{1,0:T(8,128)S(1)} %pad_maximum_fusion.1.a_ref), custom_call_target="tpu_custom_call" | custom-call | tf_op jit(solution)/shard_map/block_inverse/pallas_call | solution.py:129
  94.6 11.7 %small_inverses.1 = (f32[128,128]{1,0:T(8,128)S(1)}, f32[256,128]{1,0:T(8,128)S(1)}, f32[128,128]{1,0:T(8,128)S(1)}) custom-call(f32[128,128]{1,0:T(8,128)S(1)} %slice.20.inner_ref, f32[256,128]{1,0:T(8,128)S(1)} %get-tuple-element.16.lmt_ref, f32[256,256]{1,0:T(8,128)S(1)} %block_inverse.1.ainv_ref), custom_call_target="tpu_custom_call" | custom-call | tf_op jit(solution)/shard_map/small_inverses/pallas_call | solution.py:154
  106.2 0.0 copy-done.3
  106.2 5.9 %comp.1 = bf16[256,1536]{1,0:T(8,128)(2,1)S(1)} custom-call(f32[256,1536]{1,0:T(8,128)S(1)} %copy-done.3, f32[128,1536]{1,0:T(8,128)S(1)} %get-tuple-element.11.left_ref, f32[256,128]{1,0:T(8,128)S(1)} %get-tuple-element.16.lmt_ref, f32[256,256]{1,0:T(8,128)S(1)} %block_inverse.1.ainv_ref, f32[256,128]{1,0:T(8,128)S(1)} %get-tuple-element.12.x_ref, ...), custom_call_target="tpu_custom_call" | custom-call | tf_op jit(solution)/shard_map/comp/pallas_call | solution.py:178
  112.2 1.0 broadcast_select_fusion
  113.2 0.0 copy-done.7
  113.2 0.0 all-reduce.5.cloned.1.call-update
  113.2 0.0 all-reduce.3.cloned.1.call-start
  113.2 4.1 %dynamic-slice_select_fusion = bf16[6144,256]{1,0:T(8,128)(2,1)} fusion(bf16[6144,1536]{1,0:T(8,128)(2,1)} %w_ref.1, s32[]{:T(128)S(6)} %select_n.59, pred[]{:T(512)S(6)} %eq.7), kind=kLoop, calls=%fused_computation | loop fusion | flops 1572864 | bytes 6291461 | tf_op jit(solution)/shard_map/jit(_where)/select_n | solution.py:425
  117.3 0.0 copy-start.8
  117.3 0.0 copy-start.10
  117.4 0.0 all-reduce.3.cloned.1.call-update
  117.4 1.1 copy-done.8
  118.5 0.5 copy-done.10
  119.0 16.9 %update.1 = f32[3072,1536]{1,0:T(8,128)} custom-call(f32[256,1536]{1,0:T(8,128)S(1)} %copy-done.10, f32[128,128]{1,0:T(8,128)S(1)} %get-tuple-element.10.inv_ref, f32[128,1536]{1,0:T(8,128)S(1)} %copy-done.8, f32[3072,1536]{1,0:T(8,128)} %h_ref.3), custom_call_target="tpu_custom_call" | custom-call | flops 3623878656 | bytes 37748736 | tf_op jit(solution)/shard_map/update/pallas_call | solution.py:367
  135.9 39.2 %all-reduce.5.cloned.1.call-done.comp_ref = bf16[256,1536]{1,0:T(8,128)(2,1)} async-done(((bf16[256,1536]{1,0:T(8,128)(2,1)}), bf16[256,1536]{1,0:T(8,128)(2,1)}) %all-reduce.5.cloned.1.call-update) | async-done | bytes 786448 | tf_op jit(solution)/shard_map/psum | solution.py:446
  175.2 80.0 %all-reduce.3.cloned.1.call-done.window_ref = bf16[6144,256]{1,0:T(8,128)(2,1)} async-done(((bf16[6144,256]{1,0:T(8,128)(2,1)}), bf16[6144,256]{1,0:T(8,128)(2,1)}) %all-reduce.3.cloned.1.call-update) | async-done | bytes 3145744 | tf_op jit(solution)/shard_map/psum | solution.py:425
  255.2 0.0 copy-start.6
  255.2 1.9 copy-done.6
  257.1 0.0 copy-start.11
  257.1 1.1 copy-done.11
  258.2 0.0 copy-start.1
  258.2 17.2 %prune.1 = bf16[6144,1536]{1,0:T(8,128)(2,1)} custom-call(bf16[6144,256]{1,0:T(8,128)(2,1)S(1)} %copy-done.6, bf16[256,1536]{1,0:T(8,128)(2,1)S(1)} %copy-done.11, bf16[6144,1536]{1,0:T(8,128)(2,1)} %w_ref.1), custom_call_target="tpu_custom_call" | custom-call | flops 4831838208 | bytes 37748736 | tf_op jit(solution)/shard_map/prune/pallas_call | solution.py:395
  275.5 0.0 copy-done.1
  (6 shorter events, 0.1 us)
Async XLA Ops:
  7.2 1.9 copy-start
  7.2 168.0 %all-reduce.5.cloned.1.call-start = ((), (), s32[]{:S(2)}) async-start(), calls=%async_computation.1 | async-start | bytes 1572864 | tf_op jit(solution)/shard_map/psum | solution.py:446
  20.2 3.0 %copy-start.4 = (f32[128,1536]{1,0:T(8,128)}, f32[128,1536]{1,0:T(8,128)S(1)}, u32[]{:S(2)}) copy-start(f32[128,1536]{1,0:T(8,128)S(1)} %left_part.1.part_ref) | copy-start | bytes 2359300
  22.0 1.1 copy-start.2
  23.2 3.0 %copy-start.5 = (f32[128,1536]{1,0:T(8,128)S(1)}, f32[128,1536]{1,0:T(8,128)}, u32[]{:S(2)}) copy-start(f32[128,1536]{1,0:T(8,128)} %copy-done.4) | copy-start | bytes 2359300
  23.2 83.0 %copy-start.3 = (f32[256,1536]{1,0:T(8,128)S(1)}, f32[256,1536]{1,0:T(8,128)}, u32[]{:S(2)}) copy-start(f32[256,1536]{1,0:T(8,128)} %copy-done.2) | copy-start | bytes 4718596
  70.3 1.1 copy-start.9
  71.5 41.7 %copy-start.7 = (f32[128,1536]{1,0:T(8,128)}, f32[128,1536]{1,0:T(8,128)S(1)}, u32[]{:S(2)}) copy-start(f32[128,1536]{1,0:T(8,128)S(1)} %get-tuple-element.11.left_ref) | copy-start | bytes 2359300
  113.2 142.0 %all-reduce.3.cloned.1.call-start = ((), (), s32[]{:S(2)}) async-start(), calls=%async_computation | async-start | bytes 6291456 | tf_op jit(solution)/shard_map/psum | solution.py:425
  117.3 1.1 copy-start.8
  117.3 1.7 copy-start.10
  255.2 1.9 copy-start.6
  257.1 1.1 copy-start.11
  258.2 17.2 %copy-start.1 = (bf16[128,12288]{1,0:T(8,128)(2,1)S(1)}, bf16[128,12288]{1,0:T(8,128)(2,1)}, u32[]{:S(2)}) copy-start(bf16[128,12288]{1,0:T(8,128)(2,1)} %param.6) | copy-start | bytes 9437188
Sparse Core Ops, SparseCore 0:
  113.3 61.8 all-reduce.4
  178.2 76.9 all-reduce.2

commit v3 on v2

--- a/solution.py
+++ b/solution.py
@@ -9,6 +9,7 @@
 
 B = 256
 NB = 128
+STEP = 32
 HIGH = lax.Precision.HIGHEST
 VMEM_LIMIT = 48 * 1024 * 1024
 
@@ -37,13 +38,6 @@
     hi = x.astype(jnp.bfloat16)
     lo = (x - hi.astype(jnp.float32)).astype(jnp.bfloat16)
     return hi, lo
-
-
-def split3(x):
-    hi = x.astype(jnp.bfloat16)
-    rest = x - hi.astype(jnp.float32)
-    mid = rest.astype(jnp.bfloat16)
-    return hi, mid, (rest - mid.astype(jnp.float32)).astype(jnp.bfloat16)
 
 
 def tile_of(n, most):
@@ -59,8 +53,8 @@
         out_ref[...] = jnp.zeros_like(out_ref)
 
     c = calib_ref[...]
-    hi, mid, lo = split3(h_ref[...])
-    out_ref[...] += bf_dot(c, hi) + (bf_dot(c, mid) + bf_dot(c, lo))
+    hi, lo = split2(h_ref[...])
+    out_ref[...] += bf_dot(c, hi) + bf_dot(c, lo)
 
 
 def left_call(calib_rows, h):
@@ -78,13 +72,13 @@
         out_shape=jax.ShapeDtypeStruct((cal, cols), jnp.float32),
         compiler_params=params("arbitrary"),
         cost_estimate=pl.CostEstimate(
-            flops=6 * cal * rows * cols, bytes_accessed=4 * rows * cols, transcendentals=0
+            flops=4 * cal * rows * cols, bytes_accessed=4 * rows * cols, transcendentals=0
         ),
         name="left_part",
     )(calib_rows, h)
 
 
-def inverses(mats):
+def inverses(mats, out):
     n = NB
     ri = lax.broadcasted_iota(jnp.int32, (n, n), 0)
     ci = lax.broadcasted_iota(jnp.int32, (n, n), 1)
@@ -105,62 +99,45 @@
             row = (row + jnp.where(ck == k, 1.0, 0.0)) * inv
             col = col - jnp.where(rk == k, 1.0, 0.0)
             ms[i] = m - col * row
-    return [m * a * b for m, (a, b) in zip(ms, scales)]
-
-
-def block_inverse_kernel(a_ref, out_ref):
+        if k % STEP == STEP - 1:
+            yield
+    for m, (a, b) in zip(ms, scales):
+        m = m * a * b
+        out.append(0.5 * (m + m.T))
+
+
+def small_work(g_ref, ainv_ref, inv_ref, x_ref, sinv_ref):
     n = NB
-    a = a_ref[...]
-    a = 0.5 * (a + a.T)
-    a11, a21, a22 = a[:n, :n], a[n:, :n], a[n:, n:]
-    (p,) = inverses([a11])
-    p = 0.5 * (p + p.T)
-    w = dot(a21, p)
-    (q,) = inverses([a22 - dot_t(w, a21)])
-    q = 0.5 * (q + q.T)
-    off = -dot(q, w)
-    out_ref[:n, :n] = p - dot(w.T, off)
-    out_ref[n:, :n] = off
-    out_ref[:n, n:] = off.T
-    out_ref[n:, n:] = q
-
-
-def block_inverse(a):
-    return pl.pallas_call(
-        block_inverse_kernel,
-        out_shape=jax.ShapeDtypeStruct(a.shape, jnp.float32),
-        compiler_params=params(),
-        name="block_inverse",
-    )(a)
-
-
-def small_kernel(inner_ref, lmt_ref, ainv_ref, inv_ref, x_ref, sinv_ref):
-    inner = inner_ref[...]
+    cal = inv_ref.shape[0]
+    inner = g_ref[0:cal]
     ri = lax.broadcasted_iota(jnp.int32, inner.shape, 0)
     ci = lax.broadcasted_iota(jnp.int32, inner.shape, 1)
     inner = jnp.where(ri == ci, 1.0, 0.0) + 0.5 * (inner + inner.T)
-    lmt = lmt_ref[...]
+    base = cal + 2 * n
+    a11 = g_ref[base : base + n]
+    a21 = 0.5 * (g_ref[base + n : base + 2 * n] + g_ref[base + 2 * n : base + 3 * n].T)
+    a22 = g_ref[base + 3 * n : base + 4 * n]
+    out = []
+    yield from inverses([0.5 * (a11 + a11.T)], out)
+    p = out[0]
+    w = dot(a21, p)
+    q = 0.5 * (a22 + a22.T) - dot_t(w, a21)
+    out = []
+    yield from inverses([0.5 * (q + q.T), inner], out)
+    q, inv = out
+    inv_ref[...] = inv
+    off = -dot(q, w)
+    ainv_ref[:n, :n] = p - dot(w.T, off)
+    ainv_ref[n:, :n] = off
+    ainv_ref[:n, n:] = off.T
+    ainv_ref[n:, n:] = q
+    lmt = g_ref[cal:base]
     x = dot(ainv_ref[...], lmt)
-    s = inner - dot(lmt.T, x)
-    s = 0.5 * (s + s.T)
-    a, b = inverses([inner, s])
-    inv_ref[...] = 0.5 * (a + a.T)
-    sinv_ref[...] = 0.5 * (b + b.T)
     x_ref[...] = x
-
-
-def small(inner, lmt, ainv):
-    f = jnp.float32
-    return pl.pallas_call(
-        small_kernel,
-        out_shape=(
-            jax.ShapeDtypeStruct(inner.shape, f),
-            jax.ShapeDtypeStruct(lmt.shape, f),
-            jax.ShapeDtypeStruct(inner.shape, f),
-        ),
-        compiler_params=params(),
-        name="small_inverses",
-    )(inner, lmt, ainv)
+    sq = inner - dot(lmt.T, x)
+    out = []
+    yield from inverses([0.5 * (sq + sq.T)], out)
+    sinv_ref[...] = out[0]
 
 
 def comp_kernel(hm_ref, left_ref, lmt_ref, ainv_ref, x_ref, sinv_ref, out_ref):
@@ -187,8 +164,9 @@
 
 
 def exchange_kernel(
-    nr, nc, n, g_ref, part_ref, gout, left, right, gbuf, gsum, gbuf2, lbuf,
-    g1s, g1r, g2s, g2r, g3s, g3r, l1s, l1r, l2s, l2r, cs, cr, ss, sr,
+    nr, nc, n, g_ref, part_ref, strip_ref, gout, left, right, hm, ainv, inv, x_out, sinv,
+    gbuf, gsum, gbuf2, lbuf, hbuf,
+    g1s, g1r, g2s, g2r, g3s, g3r, l1s, l1r, l2s, l2r, cs, cr, ss, sr, h1s, h1r, h2s, h2r,
 ):
     r = lax.axis_index("row")
     c = lax.axis_index("col")
@@ -196,6 +174,7 @@
     ch = g_ref.shape[0] // nc
     cal = part_ref.shape[0]
     lc = cal // nr
+    hc = strip_ref.shape[0] // nr
 
     def send(src, dst, s, v, axis, peer):
         return pltpu.make_async_remote_copy(
@@ -223,7 +202,7 @@
     def part_rows(ref, i, size, base=0):
         return ref.at[pl.ds(pl.multiple_of(base + i * size, 8), size)]
 
-    l1, l2, g1, g2, g3 = [], [], [], [], []
+    l1, l2, g1, g2, g3, h1, h2 = [], [], [], [], [], [], []
     for d in range(1, nr):
         p = row_peer(d)
         l1.append(send(part_rows(part_ref, p, lc), lbuf.at[d], l1s.at[d], l1r.at[d], "row", p))
@@ -232,6 +211,10 @@
         p = col_peer(d)
         g1.append(send(part_rows(g_ref, p, ch), gbuf.at[d], g1s.at[d], g1r.at[d], "col", p))
         g1[-1].start()
+    for d in range(1, nr):
+        p = row_peer(d)
+        h1.append(send(part_rows(strip_ref, p, hc), hbuf.at[d], h1s.at[d], h1r.at[d], "row", p))
+        h1[-1].start()
 
     for x in g1:
         x.wait_recv()
@@ -255,6 +238,42 @@
         l2.append(send(own, own, l2s.at[d], l2r.at[d], "row", row_peer(d)))
         l2[-1].start()
 
+    up, down = lax.rem(c + n, nc), lax.rem(c + nc - n, nc)
+    origin = grp == r
+    other = jnp.logical_not(origin)
+    to_up = jnp.logical_and(grp >= r, grp + 1 < ng)
+    to_down = jnp.logical_and(grp <= r, grp > 0)
+    sends = []
+
+    def hand_on(d, at_origin):
+        chunk = lax.rem(r + nr - d, nr)
+        there = part_rows(right, chunk, lc, lane * cal)
+        u = send(there, there, cs.at[0, d], cr.at[d], "col", up)
+        w = send(there, there, cs.at[1, d], cr.at[d], "col", down)
+        near = [
+            send(there, there, ss.at[e, d], sr.at[e, d], "col", grp * n + lax.rem(lane + e, n))
+            for e in range(1, n)
+        ]
+
+        @pl.when(origin if at_origin else other)
+        def _():
+            if at_origin:
+                if d > 0:
+                    l2[d - 1].wait_recv()
+                rows_in = pl.ds(pl.multiple_of(chunk * lc, 8), lc)
+                rows_out = pl.ds(pl.multiple_of(lane * cal + chunk * lc, 8), lc)
+                right[rows_out] = left[rows_in]
+            else:
+                u.wait_recv()
+            pl.when(to_up)(u.start)
+            pl.when(to_down)(w.start)
+            for y in near:
+                y.start()
+
+        if not at_origin:
+            sends.extend([(to_up, u), (to_down, w)] + [(None, y) for y in near])
+
+    hand_on(0, True)
     for x in g2:
         x.wait_recv()
     total = gsum[...]
@@ -265,55 +284,45 @@
     for d in range(1, nc):
         g3.append(send(gown, gown, g3s.at[d], g3r.at[d], "col", col_peer(d)))
         g3[-1].start()
-
-    up, down = lax.rem(c + n, nc), lax.rem(c + nc - n, nc)
-    origin = grp == r
-    to_up = jnp.logical_and(grp >= r, grp + 1 < ng)
-    to_down = jnp.logical_and(grp <= r, grp > 0)
-
-    def sibling(e):
-        return grp * n + lax.rem(lane + e, n)
-
-    sends = []
-    for d in range(nr):
-        chunk = lax.rem(r + nr - d, nr)
-        src_left = part_rows(left, chunk, lc)
-        there = part_rows(right, chunk, lc, lane * cal)
-
-        if d > 0:
-            pl.when(origin)(l2[d - 1].wait_recv)
-
-        @pl.when(origin)
-        def _():
-            rows_in = pl.ds(pl.multiple_of(chunk * lc, 8), lc)
-            rows_out = pl.ds(pl.multiple_of(lane * cal + chunk * lc, 8), lc)
-            right[rows_out] = left[rows_in]
-
-        u = send(there, there, cs.at[0, d], cr.at[d], "col", up)
-        w = send(there, there, cs.at[1, d], cr.at[d], "col", down)
-        pl.when(jnp.logical_not(origin))(u.wait_recv)
-        pl.when(to_up)(u.start)
-        pl.when(to_down)(w.start)
-        sends += [(to_up, u), (to_down, w)]
-        for e in range(1, n):
-            x = send(there, there, ss.at[e, d], sr.at[e, d], "col", sibling(e))
-            x.start()
-            sends.append((None, x))
+    for x in g3:
+        x.wait_recv()
+
+    work = small_work(gout, ainv, inv, x_out, sinv)
+    next(work, None)
+    hand_on(0, False)
+    for d in range(1, nr):
+        hand_on(d, True)
+        next(work, None)
+        hand_on(d, False)
+        if d == nr // 2:
+            for x in h1:
+                x.wait_recv()
+            mine = pl.ds(pl.multiple_of(r * hc, 8), hc)
+            total = strip_ref[mine]
+            for e in range(1, nr):
+                total += hbuf[e]
+            hm[mine] = total
+            own = part_rows(hm, r, hc)
+            for e in range(1, nr):
+                h2.append(send(own, own, h2s.at[e], h2r.at[e], "row", row_peer(e)))
+                h2[-1].start()
+    for _ in work:
+        pass
 
     for x in l2:
-        pl.when(jnp.logical_not(origin))(x.wait_recv)
-    for x in g3:
+        pl.when(other)(x.wait_recv)
+    for x in h2:
         x.wait_recv()
     for pred, x in sends:
         if pred is None:
             x.wait()
         else:
             pl.when(pred)(x.wait_send)
-    for x in l1 + l2 + g1 + g2 + g3:
+    for x in l1 + l2 + g1 + g2 + g3 + h1 + h2:
         x.wait_send()
 
 
-def exchange(nr, nc, n, g, part):
+def exchange(nr, nc, n, g, part, strip):
     f = jnp.float32
     dma = lambda *shape: pltpu.SemaphoreType.DMA(shape)
     cal, cols = part.shape
@@ -321,27 +330,36 @@
     vmem = pl.BlockSpec(memory_space=pltpu.VMEM)
     return pl.pallas_call(
         functools.partial(exchange_kernel, nr, nc, n),
-        in_specs=[vmem, vmem],
-        out_specs=[vmem, vmem, vmem],
+        in_specs=[vmem] * 3,
+        out_specs=[vmem] * 8,
         out_shape=(
             jax.ShapeDtypeStruct(g.shape, f),
             jax.ShapeDtypeStruct(part.shape, f),
             jax.ShapeDtypeStruct((n * cal, cols), f),
+            jax.ShapeDtypeStruct(strip.shape, f),
+            jax.ShapeDtypeStruct((B, B), f),
+            jax.ShapeDtypeStruct((cal, cal), f),
+            jax.ShapeDtypeStruct((B, cal), f),
+            jax.ShapeDtypeStruct((cal, cal), f),
         ),
         scratch_shapes=[
             pltpu.VMEM((nc, ch, g.shape[1]), f),
             pltpu.VMEM((ch, g.shape[1]), f),
             pltpu.VMEM((nr, ch, g.shape[1]), f),
             pltpu.VMEM((nr, cal // nr, cols), f),
+            pltpu.VMEM((nr, B // nr, cols), f),
             dma(nc), dma(nc), dma(nr), dma(nr), dma(nc), dma(nc),
             dma(nr), dma(nr), dma(nr), dma(nr),
-            dma(2, nr), dma(nr), dma(n, nr), dma(n, nr),
+            dma(2, nr), dma(nr), dma(n, nr), dma(n, nr), dma(nr), dma(nr), dma(nr), dma(nr),
         ],
         compiler_params=pltpu.CompilerParams(
             collective_id=0, has_side_effects=True, vmem_limit_bytes=VMEM_LIMIT
         ),
+        cost_estimate=pl.CostEstimate(
+            flops=20 * cal * cols * B, bytes_accessed=64 * B * cols * 4, transcendentals=0
+        ),
         name="exchange",
-    )(g, part)
+    )(g, part, strip)
 
 
 def update_kernel(right_ref, inv_ref, left_ref, h_ref, out_ref, s_ref):
@@ -362,7 +380,7 @@
 def update_call(right, inv, left, h):
     cal = left.shape[0]
     rows, cols = h.shape
-    t = tile_of(cols, 512)
+    t = tile_of(cols, 256)
     per = cols // t
     return pl.pallas_call(
         update_kernel,
@@ -391,7 +409,7 @@
 
 def prune_call(window, comp, w):
     rows, cols = w.shape
-    t = tile_of(rows, 768)
+    t = tile_of(rows, 512)
     return pl.pallas_call(
         prune_kernel,
         grid=(rows // t,),
@@ -422,7 +440,7 @@
     off_row, off_col = start - owner_row * rows, start - owner_col * cols
 
     win = lax.dynamic_slice_in_dim(w, off_col, B, 1)
-    window = lax.psum(jnp.where(mine_col, win, jnp.zeros_like(win)), "col")
+    win = jnp.where(mine_col, win, jnp.zeros_like(win))
 
     strip = lax.dynamic_slice_in_dim(h, off_row, B, 0)
     strip = jnp.where(mine_row, strip, 0.0)
@@ -436,14 +454,14 @@
     both = dot_t(jnp.concatenate([part, strip], axis=0), calib_cols)
     g = jnp.concatenate([both, square[:, :NB], square[:, NB:]], axis=0)
 
-    g, left, right = exchange(lax.axis_size("row"), lax.axis_size("col"), rows // cols, g, part)
-    inner, lmt = g[:cal], g[cal : cal + B]
-    square = jnp.concatenate([g[cal + B : cal + 2 * B], g[cal + 2 * B :]], axis=1)
-
-    ainv = block_inverse(square)
-    inv, x, sinv = small(inner, lmt, ainv)
-    comp = comp_call(strip, left, lmt, ainv, x, sinv)
-    comp = lax.psum(jnp.where(mine_row, comp, jnp.zeros_like(comp)), "row")
+    g, win = lax.optimization_barrier((g, win))
+    window = lax.psum(win, "col")
+
+    g, left, right, hm, ainv, inv, x, sinv = exchange(
+        lax.axis_size("row"), lax.axis_size("col"), rows // cols, g, part, strip
+    )
+    left, window = lax.optimization_barrier((left, window))
+    comp = comp_call(hm, left, g[cal : cal + B], ainv, x, sinv)
     updated = update_call(right, inv, left, h)
     pruned = prune_call(window, comp, w)
     return (updated, pruned)

time: 283 us -> 233 us (0.82)
  the two profiles are of different devices: /device:TPU:0 before, /device:TPU:7 now
where the time goes in v3:
time: 233 us; the launch traced here: 232 us
  Pallas kernels  193 us (83%)
  between operations  15.1 us (6%)
  local copies, waits for them, and re-layouts  14.8 us (6%)
  other arithmetic  6.45 us (3%)
  matrix products  2.78 us (1%)
    pallas_call x1, Pallas kernels, exchange(): pl.pallas_call(functools.partial(exchange_kernel, nr, nc, n), in_specs=[v...  137 us
    pallas_call x1, Pallas kernels, update_call(): pl.pallas_call(update_kernel, grid=(rows // t,), in_specs=[pl.BlockSpec((...  20.6 us
    pallas_call x1, Pallas kernels, prune_call(): pl.pallas_call(prune_kernel, grid=(rows // t,), in_specs=[pl.BlockSpec((t...  19.5 us
    unnamed x40, local copies, waits for them, and re-layouts  14.8 us
    pallas_call x1, Pallas kernels, left_call(): pl.pallas_call(left_kernel, grid=(rows // t,), in_specs=[pl.BlockSpec((ca...  9.41 us
    pallas_call x1, Pallas kernels, comp_call(): pl.pallas_call(comp_kernel, grid=(cols // t,), in_specs=[wide(hm), wide(l...  5.92 us
  transfers between devices with their start and end apart: 1, of which 0 were waited for; matrix products, arithmetic and copies ran while one was open for 0% of the time, Pallas kernels for 59%

profile of v3, /device:TPU:7, one launch (start us, length us, event | category | flops | bytes accessed | tf_op | source)
XLA Modules:
  0.0 231.7 jit_solution(15835035592425901522)
XLA Ops:
  7.2 0.0 copy-start
  7.2 0.0 all-reduce.2.cloned.1.call-start
  8.1 1.0 copy-done
  9.1 0.1 constant_dynamic-slice_fusion.calib_ref
  9.1 9.4 %left_part.1.part_ref = f32[128,1536]{1,0:T(8,128)S(1)} custom-call(bf16[128,3072]{1,0:T(8,128)(2,1)S(1)} %constant_dynamic-slice_fusion.calib_ref, f32[3072,1536]{1,0:T(8,128)} %h_ref.3), custom_call_target="tpu_custom_call" | custom-call | flops 2415919104 | bytes 18874368 | tf_op jit(solution)/shard_map/left_part/pallas_call | solution.py:64
  18.6 0.0 copy-start.2
  18.6 0.9 copy-done.2
  19.5 1.5 dynamic-slice_select_fusion.1.strip_ref
  21.0 0.0 copy-start.19
  21.0 1.1 copy-done.19
  22.2 4.1 %dynamic-slice_select_fusion = bf16[6144,256]{1,0:T(8,128)(2,1)} fusion(bf16[6144,1536]{1,0:T(8,128)(2,1)} %w_ref.1, s32[]{:T(128)S(6)} %select_n.53, pred[]{:T(512)S(6)} %eq.7), kind=kLoop, calls=%fused_computation | loop fusion | flops 1572864 | bytes 6291461 | tf_op jit(solution)/shard_map/jit(_where)/select_n | solution.py:443
  26.3 2.8 %fusion = f32[384,128]{1,0:T(8,128)S(1)} fusion(f32[256,1536]{1,0:T(8,128)} %copy-done.19, f32[128,1536]{1,0:T(8,128)} %copy-done.2, bf16[128,12288]{1,0:T(8,128)(2,1)S(1)} %copy-done, s32[]{:T(128)S(6)} %select_n.50), kind=kOutput, calls=%fused_computation.1 | convolution fusion | flops 906559488 | bytes 2949124 | tf_op jit(solution)/shard_map/dot_general | solution.py:28
  29.1 0.8 pad_maximum_fusion.g_ref
  29.9 0.0 all-reduce.2.cloned.1.call-update
  29.9 0.0 copy-start.3
  29.9 1.1 copy-done.3
  31.0 0.0 copy-start.12
  31.0 1.0 copy-done.12
  32.0 137.1 %exchange.1 = (f32[896,128]{1,0:T(8,128)S(1)}, f32[128,1536]{1,0:T(8,128)S(1)}, f32[256,1536]{1,0:T(8,128)S(1)}, f32[256,1536]{1,0:T(8,128)S(1)}, f32[256,256]{1...) custom-call(f32[896,128]{1,0:T(8,128)S(1)} %copy-done.12, ...), custom_call_target="tpu_custom_call" | custom-call | flops 1006632960 | bytes 100663296 | tf_op jit(solution)/shard_map/exchange/pallas_call | solution.py:331
  169.1 0.0 copy-start.5
  169.1 0.9 copy-done.5
  170.0 0.0 copy-start.8
  170.0 1.1 copy-done.8
  171.2 0.0 copy-start.10
  171.2 1.2 copy-done.10
  172.3 0.0 copy-start.13
  172.3 0.7 copy-done.13
  173.0 0.0 copy-start.15
  173.0 0.6 copy-done.15
  173.6 0.0 copy-start.17
  173.6 0.6 copy-done.17
  174.3 0.0 all-reduce.2.cloned.1.call-done.window_ref
  174.3 0.0 copy-start.4
  174.3 0.0 copy-start.6
  174.3 1.3 copy-done.6
  175.6 0.0 copy-start.11
  175.6 1.4 copy-done.11
  177.0 0.0 copy-start.14
  177.0 0.9 copy-done.14
  177.9 0.0 copy-start.18
  177.9 0.8 copy-done.18
  178.7 5.9 %comp.1.comp_ref = bf16[256,1536]{1,0:T(8,128)(2,1)S(1)} custom-call(f32[256,1536]{1,0:T(8,128)S(1)} %copy-done.11, f32[128,1536]{1,0:T(8,128)S(1)} %copy-done.6, f32[256,128]{1,0:T(8,128)S(1)} %slice.11.lmt_ref, f32[256,256]{1,0:T(8,128)S(1)} %get-tuple-element.23.ainv_ref, f32[256,128]{1,0:T(8,128)S(1)} %copy-done.14, f32[128,128]{1,0:T(8,128)S(1)} %copy-done.18), custom_call_target="tpu_custom_call" | custom-call | tf_op jit(solution)/shard_map/comp/pallas_call | solution.py:155
  184.7 0.0 copy-done.4
  184.7 0.0 copy-start.7
  184.7 0.0 copy-start.9
  184.7 0.0 copy-start.16
  184.7 19.5 %prune.1 = bf16[6144,1536]{1,0:T(8,128)(2,1)} custom-call(bf16[6144,256]{1,0:T(8,128)(2,1)S(1)} %copy-done.4, bf16[256,1536]{1,0:T(8,128)(2,1)S(1)} %comp.1.comp_ref, bf16[6144,1536]{1,0:T(8,128)(2,1)} %w_ref.1), custom_call_target="tpu_custom_call" | custom-call | flops 4831838208 | bytes 37748736 | tf_op jit(solution)/shard_map/prune/pallas_call | solution.py:413
  204.2 0.0 copy-done.7
  204.2 0.0 copy-done.9
  204.2 0.0 copy-done.16
  204.2 0.0 copy-start.1
  204.3 20.6 %update.1 = f32[3072,1536]{1,0:T(8,128)} custom-call(f32[256,1536]{1,0:T(8,128)S(1)} %copy-done.9, f32[128,128]{1,0:T(8,128)S(1)} %copy-done.16, f32[128,1536]{1,0:T(8,128)S(1)} %copy-done.7, f32[3072,1536]{1,0:T(8,128)} %h_ref.3), custom_call_target="tpu_custom_call" | custom-call | flops 3623878656 | bytes 37748736 | tf_op jit(solution)/shard_map/update/pallas_call | solution.py:385
  224.9 0.0 copy-done.1
  (3 shorter events, 0.0 us)
Async XLA Ops:
  7.2 1.9 copy-start
  7.2 167.1 %all-reduce.2.cloned.1.call-start = ((), (), s32[]{:S(2)}) async-start(), calls=%async_computation | async-start | bytes 6291456 | tf_op jit(solution)/shard_map/psum | solution.py:458
  18.6 0.9 copy-start.2
  21.0 1.1 copy-start.19
  29.9 1.1 copy-start.3
  31.0 1.0 copy-start.12
  169.1 0.9 copy-start.5
  170.0 1.1 copy-start.8
  171.2 1.2 copy-start.10
  172.3 0.7 copy-start.13
  173.0 0.6 copy-start.15
  173.6 0.6 copy-start.17
  174.3 10.4 %copy-start.4 = (bf16[6144,256]{1,0:T(8,128)(2,1)S(1)}, bf16[6144,256]{1,0:T(8,128)(2,1)}, u32[]{:S(2)}) copy-start(bf16[6144,256]{1,0:T(8,128)(2,1)} %all-reduce.2.cloned.1.call-done.window_ref) | copy-start | bytes 9437188
  174.3 1.3 copy-start.6
  175.6 1.4 copy-start.11
  177.0 0.9 copy-start.14
  177.9 0.8 copy-start.18
  184.7 19.5 %copy-start.7 = (f32[128,1536]{1,0:T(8,128)S(1)}, f32[128,1536]{1,0:T(8,128)}, u32[]{:S(2)}) copy-start(f32[128,1536]{1,0:T(8,128)} %copy-done.5) | copy-start | bytes 2359300
  184.7 19.5 %copy-start.9 = (f32[256,1536]{1,0:T(8,128)S(1)}, f32[256,1536]{1,0:T(8,128)}, u32[]{:S(2)}) copy-start(f32[256,1536]{1,0:T(8,128)} %copy-done.8) | copy-start | bytes 4718596
  184.7 19.5 %copy-start.16 = (f32[128,128]{1,0:T(8,128)S(1)}, f32[128,128]{1,0:T(8,128)}, u32[]{:S(2)}) copy-start(f32[128,128]{1,0:T(8,128)} %copy-done.15) | copy-start | bytes 196612
  204.2 20.7 %copy-start.1 = (bf16[128,12288]{1,0:T(8,128)(2,1)S(1)}, bf16[128,12288]{1,0:T(8,128)(2,1)}, u32[]{:S(2)}) copy-start(bf16[128,12288]{1,0:T(8,128)(2,1)} %param.6) | copy-start | bytes 9437188
Sparse Core Ops, SparseCore 0:
  30.0 110.5 all-reduce.1

commit v4 on v3

--- a/solution.py
+++ b/solution.py
@@ -10,6 +10,7 @@
 B = 256
 NB = 128
 STEP = 32
+PIECES = 8
 HIGH = lax.Precision.HIGHEST
 VMEM_LIMIT = 48 * 1024 * 1024
 
@@ -164,9 +165,10 @@
 
 
 def exchange_kernel(
-    nr, nc, n, g_ref, part_ref, strip_ref, gout, left, right, hm, ainv, inv, x_out, sinv,
-    gbuf, gsum, gbuf2, lbuf, hbuf,
+    nr, nc, n, g_ref, part_ref, strip_ref, win_ref, gout, left, right, hm, ainv, inv, x_out, sinv, wout,
+    gbuf, gsum, gbuf2, lbuf, hbuf, wbuf, base, wu, wd, ru, rd,
     g1s, g1r, g2s, g2r, g3s, g3r, l1s, l1r, l2s, l2r, cs, cr, ss, sr, h1s, h1r, h2s, h2r,
+    w0s, w0r, us, ur, ds, dr, w2s, w2r,
 ):
     r = lax.axis_index("row")
     c = lax.axis_index("col")
@@ -215,6 +217,71 @@
         p = row_peer(d)
         h1.append(send(part_rows(strip_ref, p, hc), hbuf.at[d], h1s.at[d], h1r.at[d], "row", p))
         h1[-1].start()
+
+    wl = win_ref.shape[0] // n
+    wq = wl // PIECES
+    w0 = []
+    for e in range(1, n):
+        k = lax.rem(lane + e, n)
+        w0.append(
+            send(part_rows(win_ref, k, wl), wbuf.at[e], w0s.at[e], w0r.at[e], "col", grp * n + k)
+        )
+        w0[-1].start()
+    has_up, has_down = grp + 1 < ng, grp > 0
+    next_up, next_down = lax.rem(c + n, nc), lax.rem(c + nc - n, nc)
+    wsends = []
+    steps = PIECES + ng - 1
+
+    def window_up(q):
+        piece = pl.ds(pl.multiple_of(q * wq, 16), wq)
+        return piece, send(wu.at[piece], ru.at[piece], us.at[q], ur.at[q], "col", next_up)
+
+    def window_down(q):
+        piece = pl.ds(pl.multiple_of(q * wq, 16), wq)
+        return piece, send(wd.at[piece], rd.at[piece], ds.at[q], dr.at[q], "col", next_down)
+
+    def pass_window(t):
+        for q, make, out, came, has_in, has_out in (
+            (t - grp, window_up, wu, ru, has_down, has_up),
+            (t - (ng - 1 - grp), window_down, wd, rd, has_up, has_down),
+        ):
+
+            @pl.when(jnp.logical_and(q >= 0, q < PIECES))
+            def _():
+                piece, x = make(q)
+
+                @pl.when(has_in)
+                def _():
+                    x.wait_recv()
+                    out[piece] = base[piece] + came[piece]
+
+                @pl.when(jnp.logical_not(has_in))
+                def _():
+                    out[piece] = base[piece]
+
+                pl.when(has_out)(x.start)
+
+    def finish_window():
+        there = pl.ds(pl.multiple_of(lane * wl, 16), wl)
+
+        @pl.when(has_down)
+        def _():
+            base[...] = base[...] + ru[...]
+
+        @pl.when(has_up)
+        def _():
+            base[...] = base[...] + rd[...]
+
+        wout[there] = base[...]
+        for e in range(1, n):
+            y = send(
+                wout.at[there], wout.at[there], w2s.at[e], w2r.at[e], "col",
+                grp * n + lax.rem(lane + e, n),
+            )
+            y.start()
+            wsends.append((None, y))
+        for q in range(PIECES):
+            wsends.extend([(has_up, window_up(q)[1]), (has_down, window_down(q)[1])])
 
     for x in g1:
         x.wait_recv()
@@ -284,16 +351,28 @@
     for d in range(1, nc):
         g3.append(send(gown, gown, g3s.at[d], g3r.at[d], "col", col_peer(d)))
         g3[-1].start()
+    for x in w0:
+        x.wait_recv()
+    share = win_ref[pl.ds(pl.multiple_of(lane * wl, 16), wl)]
+    for e in range(1, n):
+        share += wbuf[e]
+    base[...] = share
+    pass_window(0)
     for x in g3:
         x.wait_recv()
 
     work = small_work(gout, ainv, inv, x_out, sinv)
     next(work, None)
     hand_on(0, False)
+    passed = 1
     for d in range(1, nr):
         hand_on(d, True)
         next(work, None)
         hand_on(d, False)
+        while passed < 1 + (steps - 1) * d // (nr - 1):
+            next(work, None)
+            pass_window(passed)
+            passed += 1
         if d == nr // 2:
             for x in h1:
                 x.wait_recv()
@@ -306,6 +385,7 @@
             for e in range(1, nr):
                 h2.append(send(own, own, h2s.at[e], h2r.at[e], "row", row_peer(e)))
                 h2[-1].start()
+    finish_window()
     for _ in work:
         pass
 
@@ -313,25 +393,26 @@
         pl.when(other)(x.wait_recv)
     for x in h2:
         x.wait_recv()
-    for pred, x in sends:
+    for pred, x in sends + wsends:
         if pred is None:
             x.wait()
         else:
             pl.when(pred)(x.wait_send)
-    for x in l1 + l2 + g1 + g2 + g3 + h1 + h2:
+    for x in l1 + l2 + g1 + g2 + g3 + h1 + h2 + w0:
         x.wait_send()
 
 
-def exchange(nr, nc, n, g, part, strip):
+def exchange(nr, nc, n, g, part, strip, win):
     f = jnp.float32
     dma = lambda *shape: pltpu.SemaphoreType.DMA(shape)
     cal, cols = part.shape
     ch = g.shape[0] // nc
+    wl = win.shape[0] // n
     vmem = pl.BlockSpec(memory_space=pltpu.VMEM)
     return pl.pallas_call(
         functools.partial(exchange_kernel, nr, nc, n),
-        in_specs=[vmem] * 3,
-        out_specs=[vmem] * 8,
+        in_specs=[vmem] * 4,
+        out_specs=[vmem] * 9,
         out_shape=(
             jax.ShapeDtypeStruct(g.shape, f),
             jax.ShapeDtypeStruct(part.shape, f),
@@ -341,6 +422,7 @@
             jax.ShapeDtypeStruct((cal, cal), f),
             jax.ShapeDtypeStruct((B, cal), f),
             jax.ShapeDtypeStruct((cal, cal), f),
+            jax.ShapeDtypeStruct(win.shape, win.dtype),
         ),
         scratch_shapes=[
             pltpu.VMEM((nc, ch, g.shape[1]), f),
@@ -348,9 +430,12 @@
             pltpu.VMEM((nr, ch, g.shape[1]), f),
             pltpu.VMEM((nr, cal // nr, cols), f),
             pltpu.VMEM((nr, B // nr, cols), f),
+            pltpu.VMEM((n, wl, win.shape[1]), win.dtype),
+            *[pltpu.VMEM((wl, win.shape[1]), win.dtype)] * 5,
             dma(nc), dma(nc), dma(nr), dma(nr), dma(nc), dma(nc),
             dma(nr), dma(nr), dma(nr), dma(nr),
             dma(2, nr), dma(nr), dma(n, nr), dma(n, nr), dma(nr), dma(nr), dma(nr), dma(nr),
+            dma(n), dma(n), *[dma(PIECES)] * 4, dma(n), dma(n),
         ],
         compiler_params=pltpu.CompilerParams(
             collective_id=0, has_side_effects=True, vmem_limit_bytes=VMEM_LIMIT
@@ -359,7 +444,7 @@
             flops=20 * cal * cols * B, bytes_accessed=64 * B * cols * 4, transcendentals=0
         ),
         name="exchange",
-    )(g, part, strip)
+    )(g, part, strip, win)
 
 
 def update_kernel(right_ref, inv_ref, left_ref, h_ref, out_ref, s_ref):
@@ -380,7 +465,7 @@
 def update_call(right, inv, left, h):
     cal = left.shape[0]
     rows, cols = h.shape
-    t = tile_of(cols, 256)
+    t = tile_of(cols, 768)
     per = cols // t
     return pl.pallas_call(
         update_kernel,
@@ -409,7 +494,7 @@
 
 def prune_call(window, comp, w):
     rows, cols = w.shape
-    t = tile_of(rows, 512)
+    t = tile_of(rows, 1536)
     return pl.pallas_call(
         prune_kernel,
         grid=(rows // t,),
@@ -454,13 +539,9 @@
     both = dot_t(jnp.concatenate([part, strip], axis=0), calib_cols)
     g = jnp.concatenate([both, square[:, :NB], square[:, NB:]], axis=0)
 
-    g, win = lax.optimization_barrier((g, win))
-    window = lax.psum(win, "col")
-
-    g, left, right, hm, ainv, inv, x, sinv = exchange(
-        lax.axis_size("row"), lax.axis_size("col"), rows // cols, g, part, strip
+    g, left, right, hm, ainv, inv, x, sinv, window = exchange(
+        lax.axis_size("row"), lax.axis_size("col"), rows // cols, g, part, strip, win
     )
-    left, window = lax.optimization_barrier((left, window))
     comp = comp_call(hm, left, g[cal : cal + B], ainv, x, sinv)
     updated = update_call(right, inv, left, h)
     pruned = prune_call(window, comp, w)

time: 233 us -> 218 us (0.936)
  the two profiles are of different devices: /device:TPU:7 before, /device:TPU:0 now
where the time goes in v4:
time: 218 us; the launch traced here: 216 us
  Pallas kernels  206 us (94%)
  other arithmetic  5.69 us (3%)
    pallas_call x1, Pallas kernels, exchange(): pl.pallas_call(functools.partial(exchange_kernel, nr, nc, n), in_specs=[v...  161 us
    pallas_call x1, Pallas kernels, update_call(): pl.pallas_call(update_kernel, grid=(rows // t,), in_specs=[pl.BlockSpec((...  15.5 us
    pallas_call x1, Pallas kernels, prune_call(): pl.pallas_call(prune_kernel, grid=(rows // t,), in_specs=[pl.BlockSpec((t...  14.5 us
    pallas_call x1, Pallas kernels, left_call(): pl.pallas_call(left_kernel, grid=(rows // t,), in_specs=[pl.BlockSpec((ca...  9.41 us
    pallas_call x1, Pallas kernels, comp_call(): pl.pallas_call(comp_kernel, grid=(cols // t,), in_specs=[wide(hm), wide(l...  5.94 us

profile of v4, /device:TPU:0, one launch (start us, length us, event | category | flops | bytes accessed | tf_op | source)
XLA Modules:
  0.0 215.9 jit_solution(8019275046225935676)
XLA Ops:
  0.6 0.0 copy-start
  1.5 1.0 copy-done
  2.5 0.1 constant_dynamic-slice_fusion.calib_ref
  2.6 9.4 %left_part.1.part_ref = f32[128,1536]{1,0:T(8,128)S(1)} custom-call(bf16[128,3072]{1,0:T(8,128)(2,1)S(1)} %constant_dynamic-slice_fusion.calib_ref, f32[3072,1536]{1,0:T(8,128)} %h_ref.3), custom_call_target="tpu_custom_call" | custom-call | flops 2415919104 | bytes 18874368 | tf_op jit(solution)/shard_map/left_part/pallas_call | solution.py:65
  12.0 1.5 dynamic-slice_select_fusion.1.strip_ref
  13.5 0.0 copy-start.3
  13.6 1.2 fusion
  14.9 4.1 %dynamic-slice_select_fusion.win_ref = bf16[6144,256]{1,0:T(8,128)(2,1)} fusion(bf16[6144,1536]{1,0:T(8,128)(2,1)} %w_ref.1, s32[]{:T(128)S(6)} %select_n.53, pred[]{:T(512)S(6)} %eq.7), kind=kLoop, calls=%fused_computation | loop fusion | flops 1572864 | bytes 6291461 | tf_op jit(solution)/shard_map/jit(_where)/select_n | solution.py:528
  19.0 0.0 copy-done.3
  19.0 160.9 %exchange.1 = (f32[896,128]{1,0:T(8,128)S(1)}, f32[128,1536]{1,0:T(8,128)S(1)}, f32[256,1536]{1,0:T(8,128)S(1)}, f32[256,1536]{1,0:T(8,128)S(1)}, f32[256,256]{1...) custom-call(f32[896,128]{1,0:T(8,128)S(1)} %pad_maximum_fusion.g_ref, ...), custom_call_target="tpu_custom_call" | custom-call | flops 1006632960 | bytes 100663296 | tf_op jit(solution)/shard_map/exchange/pallas_call | solution.py:412
  179.9 0.0 copy-start.2
  180.0 5.9 %comp.1.comp_ref = bf16[256,1536]{1,0:T(8,128)(2,1)S(1)} custom-call(f32[256,1536]{1,0:T(8,128)S(1)} %get-tuple-element.15.hm_ref, f32[128,1536]{1,0:T(8,128)S(1)} %get-tuple-element.13.left_ref, f32[256,128]{1,0:T(8,128)S(1)} %slice.11.lmt_ref, f32[256,256]{1,0:T(8,128)S(1)} %get-tuple-element.17.ainv_ref, f32[256,128]{1,0:T(8,128)S(1)} %get-tuple-element.18.x_ref, ...), custom_call_target="tpu_custom_call" | custom-call | tf_op jit(solution)/shard_map/comp/pallas_call | solution.py:156
  185.9 0.0 copy-done.2
  185.9 14.5 %prune.1 = bf16[6144,1536]{1,0:T(8,128)(2,1)} custom-call(bf16[6144,256]{1,0:T(8,128)(2,1)S(1)} %copy-done.2, bf16[256,1536]{1,0:T(8,128)(2,1)S(1)} %comp.1.comp_ref, bf16[6144,1536]{1,0:T(8,128)(2,1)} %w_ref.1), custom_call_target="tpu_custom_call" | custom-call | flops 4831838208 | bytes 37748736 | tf_op jit(solution)/shard_map/prune/pallas_call | solution.py:498
  200.4 0.0 copy-start.1
  200.4 15.5 %update.1 = f32[3072,1536]{1,0:T(8,128)} custom-call(f32[256,1536]{1,0:T(8,128)S(1)} %get-tuple-element.11.right_ref, f32[128,128]{1,0:T(8,128)S(1)} %get-tuple-element.12.inv_ref, f32[128,1536]{1,0:T(8,128)S(1)} %get-tuple-element.13.left_ref, f32[3072,1536]{1,0:T(8,128)} %h_ref.3), custom_call_target="tpu_custom_call" | custom-call | flops 3623878656 | bytes 37748736 | tf_op jit(solution)/shard_map/update/pallas_call | solution.py:470
  215.9 0.0 copy-done.1
  (4 shorter events, 0.1 us)
Async XLA Ops:
  0.6 1.9 copy-start
  13.5 5.4 %copy-start.3 = (f32[256,1536]{1,0:T(8,128)}, f32[256,1536]{1,0:T(8,128)S(1)}, u32[]{:S(2)}) copy-start(f32[256,1536]{1,0:T(8,128)S(1)} %dynamic-slice_select_fusion.1.strip_ref) | copy-start | bytes 4718596
  179.9 6.0 %copy-start.2 = (bf16[6144,256]{1,0:T(8,128)(2,1)S(1)}, bf16[6144,256]{1,0:T(8,128)(2,1)}, u32[]{:S(2)}) copy-start(bf16[6144,256]{1,0:T(8,128)(2,1)} %get-tuple-element.14.window_ref) | copy-start | bytes 9437188
  200.4 15.5 %copy-start.1 = (bf16[128,12288]{1,0:T(8,128)(2,1)S(1)}, bf16[128,12288]{1,0:T(8,128)(2,1)}, u32[]{:S(2)}) copy-start(bf16[128,12288]{1,0:T(8,128)(2,1)} %param.6) | copy-start | bytes 9437188
